TPU v7x, 256 devices: a whole 4x4x8 slice. The times are simulated.
256 devices in a mesh: seq: 64 (over z_hi, x, y, core), head: 4 (over z_lo).
Axes of the slice: x: 4, y: 4, z: 8 (z_hi: 2, z_lo: 4; z = z_hi * 4 + z_lo), core: 2. Of those that a mesh axis runs over, the one named last changes fastest.
Arguments:
- queries: bfloat16 [16384, 4096], P('seq', 'head'), may hold values from -80 to 80
- keys: bfloat16 [16384, 4096], P('seq', 'head'), may hold values from -4 to 4
- values: bfloat16 [16384, 4096], P('seq', 'head'), may hold values from -5 to 5
- layout: int32 [128, 5], P('seq'), may hold values from 0 to 1
- out_weight: bfloat16 [4096, 4096], P('head'), may hold values from -0.125 to 0.125
- out_grad: bfloat16 [16384, 4096], P('seq', 'head'), may hold values from -5 to 5
Outputs:
- mixed: bfloat16 [16384, 4096], P('seq', 'head')
- grad_queries: bfloat16 [16384, 4096], P('seq', 'head')
- grad_keys: bfloat16 [16384, 4096], P('seq', 'head')
- grad_values: bfloat16 [16384, 4096], P('seq', 'head')
All inputs are finite; a program needn't handle non-finite values.
Results may differ from a plain program's by a relative error of at most 0.034.
Values may be sent and summed in bfloat16 or wider, within the bound.
No kernel may reach another device: no remote copies, remote signals or barrier semaphores. Data moves between devices by JAX's collectives and lax.ppermute only.
A program may use at most 128 MiB of HBM per device.

v0:
```python
import math

import jax
import jax.numpy as jnp
from jax import lax
from jax.sharding import PartitionSpec as P

HD = 128
BLOCK_TOKENS = 128
LEVELS = 5


def shifted(value, axis, steps):
    count = lax.axis_size(axis)
    initial, last = (max(0, -steps), min(count, count - steps))
    return lax.ppermute(value, axis, [(source, source + steps) for source in range(initial, last)])


def body(queries, keys, values, layout, out_weight, out_grad):
    tokens_here = queries.shape[0]
    per_device = tokens_here // BLOCK_TOKENS
    heads_here = queries.shape[1] // HD
    logit_scale = 1.0 / math.sqrt(HD)
    devices = lax.axis_size("seq")
    position = lax.axis_index("seq")
    exponents = [e for e in range(LEVELS) if 2**e < devices]
    visit_order = list(exponents)
    slots = jnp.arange(per_device, dtype=jnp.int32)

    def blocked(field):
        return field.reshape(per_device, BLOCK_TOKENS, heads_here, HD)

    def chooser(exponent, kind):
        return (layout[:, exponent][:, None] == slots[None, :]).astype(kind)

    def pick_blocks(exponent, fetched):
        chosen = jnp.einsum(
            "qc,ckd->qkd",
            chooser(exponent, jnp.bfloat16),
            fetched.reshape(per_device, BLOCK_TOKENS, -1),
            preferred_element_type=jnp.float32,
        )
        return chosen.astype(jnp.bfloat16).reshape(per_device, BLOCK_TOKENS, heads_here, HD)

    query_blocks = blocked(queries)
    key_blocks = blocked(keys)
    value_blocks = blocked(values)
    causal = jnp.tril(jnp.ones((BLOCK_TOKENS, BLOCK_TOKENS), bool))
    local_scores = (
        jnp.einsum("bqhd,bkhd->bhqk", query_blocks, key_blocks, preferred_element_type=jnp.float32)
        * logit_scale
    )
    distant_keys = {}
    distant_values = {}
    distant_scores = {}
    for exponent in visit_order:
        fetched_keys, fetched_values = shifted((keys, values), "seq", 2**exponent)
        distant_keys[exponent] = pick_blocks(exponent, fetched_keys)
        distant_values[exponent] = pick_blocks(exponent, fetched_values)
        distant_scores[exponent] = (
            jnp.einsum(
                "bqhd,bkhd->bhqk",
                query_blocks,
                distant_keys[exponent],
                preferred_element_type=jnp.float32,
            )
            * logit_scale
        )
    score_parts = [local_scores] + [distant_scores[e] for e in exponents]
    allowed_parts = [jnp.broadcast_to(causal, local_scores.shape)] + [
        jnp.broadcast_to(position >= 2**e, distant_scores[e].shape) for e in exponents
    ]
    scores = jnp.concatenate(score_parts, -1)
    allowed = jnp.concatenate(allowed_parts, -1)
    row_peak = jnp.max(jnp.where(allowed, scores, -jnp.inf), -1, keepdims=True)
    weights_raw = jnp.where(allowed, jnp.exp(scores - row_peak), 0.0)
    probs = weights_raw / jnp.sum(weights_raw, -1, keepdims=True)
    probs_low = probs.astype(jnp.bfloat16)

    def portion(field, index):
        return field[..., index * BLOCK_TOKENS : (index + 1) * BLOCK_TOKENS]

    key_groups = [key_blocks] + [distant_keys[e] for e in exponents]
    value_groups = [value_blocks] + [distant_values[e] for e in exponents]
    attn_total = jnp.zeros((per_device, BLOCK_TOKENS, heads_here, HD), jnp.float32)
    for index in range(len(value_groups)):
        attn_total = attn_total + jnp.einsum(
            "bhqk,bkhd->bqhd",
            portion(probs_low, index),
            value_groups[index],
            preferred_element_type=jnp.float32,
        )
    sparse_attention = attn_total.reshape(tokens_here, -1).astype(jnp.bfloat16)
    partial_value = jnp.dot(sparse_attention, out_weight, preferred_element_type=jnp.float32)
    mixed = lax.psum_scatter(partial_value, "head", scatter_dimension=1, tiled=True).astype(
        jnp.bfloat16
    )
    full_grad = lax.all_gather(out_grad, "head", axis=1, tiled=True)
    grad_attn = jnp.einsum(
        "tc,rc->tr", full_grad, out_weight, preferred_element_type=jnp.float32
    ).astype(jnp.bfloat16)
    grad_blocks = blocked(grad_attn)
    attn_blocks = blocked(sparse_attention)
    correction = jnp.sum(
        grad_blocks.astype(jnp.float32) * attn_blocks.astype(jnp.float32), -1
    ).transpose(0, 2, 1)[..., None]
    query_gradient = jnp.zeros((per_device, BLOCK_TOKENS, heads_here, HD), jnp.float32)
    key_gradient_sum = jnp.zeros((per_device, BLOCK_TOKENS, heads_here, HD), jnp.float32)
    value_gradient_sum = jnp.zeros((per_device, BLOCK_TOKENS, heads_here, HD), jnp.float32)
    for index in [0] + [1 + exponents.index(e) for e in visit_order]:
        grad_probs = jnp.einsum(
            "bqhd,bkhd->bhqk", grad_blocks, value_groups[index], preferred_element_type=jnp.float32
        )
        grad_scores = (portion(probs, index) * (grad_probs - correction) * logit_scale).astype(
            jnp.bfloat16
        )
        query_gradient = query_gradient + jnp.einsum(
            "bhqk,bkhd->bqhd", grad_scores, key_groups[index], preferred_element_type=jnp.float32
        )
        grad_key = jnp.einsum(
            "bhqk,bqhd->bkhd", grad_scores, query_blocks, preferred_element_type=jnp.float32
        )
        grad_value = jnp.einsum(
            "bhqk,bqhd->bkhd",
            portion(probs_low, index),
            grad_blocks,
            preferred_element_type=jnp.float32,
        )
        if index == 0:
            key_gradient_sum = grad_key
            value_gradient_sum = grad_value
        else:
            exponent = exponents[index - 1]
            pick_mask = chooser(exponent, jnp.float32)[:, :, None, None, None]
            send_keys = (
                jnp.sum(pick_mask * grad_key[:, None], 0)
                .astype(jnp.bfloat16)
                .reshape(tokens_here, -1)
            )
            send_values = (
                jnp.sum(pick_mask * grad_value[:, None], 0)
                .astype(jnp.bfloat16)
                .reshape(tokens_here, -1)
            )
            back_keys, back_values = shifted((send_keys, send_values), "seq", -(2**exponent))
            key_gradient_sum = key_gradient_sum + blocked(back_keys).astype(jnp.float32)
            value_gradient_sum = value_gradient_sum + blocked(back_values).astype(jnp.float32)
    return (
        mixed,
        query_gradient.reshape(tokens_here, -1).astype(jnp.bfloat16),
        key_gradient_sum.reshape(tokens_here, -1).astype(jnp.bfloat16),
        value_gradient_sum.reshape(tokens_here, -1).astype(jnp.bfloat16),
    )


def solution(mesh):
    placed = (
        P("seq", "head"),
        P("seq", "head"),
        P("seq", "head"),
        P("seq", None),
        P("head", None),
        P("seq", "head"),
    )
    return jax.shard_map(
        body,
        mesh=mesh,
        in_specs=placed,
        out_specs=(P("seq", "head"), P("seq", "head"), P("seq", "head"), P("seq", "head")),
        check_vma=False,
    )
```

profile of v0, /device:TPU:63, one launch (start us, length us, event | category | flops | bytes accessed | tf_op | source)
XLA Modules:
  0.0 544.0 jit_solution(13758213080107092689)
XLA Ops:
  7.2 8.2 %collective-permute-start = (bf16[256,1024]{1,0:T(8,128)(2,1)}, bf16[256,1024]{1,0:T(8,128)(2,1)}, u32[]{:S(2)}, u32[]{:S(2)}) collective-permute-start(bf16[256,1024]{1,0:T(8,128)(2,1)} %param.7), channel_id=1, source_target_pairs={{0,4},{4,8},{8,12},{12,16},{16,20},{20,24},{24,28},{28,32},{32,36}... | collective-permute-start | bytes 1572872 | tf_op jit(solution)/shard_map/ppermute | solution.py:16
  15.4 3.2 collective-permute-start.1
  18.6 3.9 collective-permute-start.2
  22.6 3.1 collective-permute-start.3
  25.7 3.8 collective-permute-start.4
  36.0 129.0 %collective-permute-done = bf16[256,1024]{1,0:T(8,128)(2,1)} collective-permute-done((bf16[256,1024]{1,0:T(8,128)(2,1)}, bf16[256,1024]{1,0:T(8,128)(2,1)}, u32[]{:S(2)}, u32[]{:S(2)}) %collective-permute-start) | collective-permute-done | bytes 524320 | tf_op jit(solution)/shard_map/ppermute | solution.py:16
  169.3 20.4 %collective-permute-done.1 = bf16[256,1024]{1,0:T(8,128)(2,1)} collective-permute-done((bf16[256,1024]{1,0:T(8,128)(2,1)}, bf16[256,1024]{1,0:T(8,128)(2,1)}, u32[]{:S(2)}, u32[]{:S(2)}) %collective-permute-start.1) | collective-permute-done | bytes 524320 | tf_op jit(solution)/shard_map/ppermute | solution.py:16
  195.3 5.7 %collective-permute-done.2 = bf16[256,1024]{1,0:T(8,128)(2,1)S(1)} collective-permute-done((bf16[256,1024]{1,0:T(8,128)(2,1)}, bf16[256,1024]{1,0:T(8,128)(2,1)S(1)}, u32[]{:S(2)}, u32[]{:S(2)}) %collective-permute-start.2) | collective-permute-done | bytes 524320 | tf_op jit(solution)/shard_map/ppermute | solution.py:16
  201.0 12.1 %collective-permute-start.7 = (bf16[256,1024]{1,0:T(8,128)(2,1)}, bf16[256,1024]{1,0:T(8,128)(2,1)}, u32[]{:S(2)}, u32[]{:S(2)}) collective-permute-start(bf16[256,1024]{1,0:T(8,128)(2,1)} %param.8), channel_id=1, source_target_pairs={{0,16},{4,20},{8,24},{12,28},{16,32},{20,36},{24,40},{28,44},{32,4... | collective-permute-start | bytes 1572872 | tf_op jit(solution)/shard_map/ppermute | solution.py:16
  239.5 6.4 %collective-permute-done.8 = bf16[256,1024]{1,0:T(8,128)(2,1)} collective-permute-done((bf16[256,1024]{1,0:T(8,128)(2,1)}, bf16[256,1024]{1,0:T(8,128)(2,1)}, u32[]{:S(2)}, u32[]{:S(2)}) %collective-permute-start.8) | collective-permute-done | bytes 524320 | tf_op jit(solution)/shard_map/ppermute | solution.py:16
  248.6 8.6 %collective-permute-done.7 = bf16[256,1024]{1,0:T(8,128)(2,1)} collective-permute-done((bf16[256,1024]{1,0:T(8,128)(2,1)}, bf16[256,1024]{1,0:T(8,128)(2,1)}, u32[]{:S(2)}, u32[]{:S(2)}) %collective-permute-start.7) | collective-permute-done | bytes 524320 | tf_op jit(solution)/shard_map/ppermute | solution.py:16
  261.1 2.8 collective-permute-done.6
  292.8 7.1 %fusion.123 = (f32[2,8,128]{2,1,0:T(8,128)S(1)}, f32[2,8,128,768]{2,3,1,0:T(8,128)S(1)}) fusion(pred[2,8,128,768]{2,3,1,0:T(8,128)(4,1)S(1)} %copy-done.33, f32[2,8,128,768]{2,3,1,0:T(8,128)} %constant_dynamic-update-slice_fusion), kind=kOutput, calls=%fused_computation.231 | output fusion | flops 6292223 | bytes 14163968 | tf_op jit(solution)/shard_map/sub | solution.py:76
  299.9 3.8 fusion.122
  310.6 6.4 %fusion.41 = bf16[32,8,8,128]{3,1,2,0:T(8,128)(2,1)S(1)} fusion(bf16[256,4096]{1,0:T(8,128)(2,1)} %all-gather.2.cloned.1.call-done, bf16[1024,4096]{1,0:T(8,128)(2,1)} %param.10), kind=kOutput, calls=%fused_computation.99 | convolution fusion | flops 2147745792 | bytes 11010048 | tf_op jit(solution)/shard_map/tc,rc->tr/dot_general | solution.py:99
  319.3 4.1 multiply_reduce_fusion.10
  332.9 7.8 %fusion.43 = f32[256,4096]{1,0:T(8,128)} fusion(bf16[1024,4096]{1,0:T(8,128)(2,1)} %param.10, bf16[32,8,8,128]{3,2,1,0:T(8,128)(2,1)S(1)} %bitcast.333), kind=kOutput, calls=%fused_computation.131 | convolution fusion | flops 2147483648 | bytes 13107200 | tf_op jit(solution)/shard_map/dot_general | solution.py:94
  399.7 10.0 %collective-permute-done.14 = bf16[256,1024]{1,0:T(8,128)(2,1)} collective-permute-done((bf16[256,1024]{1,0:T(8,128)(2,1)}, bf16[256,1024]{1,0:T(8,128)(2,1)}, u32[]{:S(2)}, u32[]{:S(2)}) %collective-permute-start.14) | collective-permute-done | bytes 524320 | tf_op jit(solution)/shard_map/ppermute | solution.py:16
  417.6 45.0 %collective-permute-done.12 = bf16[256,1024]{1,0:T(8,128)(2,1)} collective-permute-done((bf16[256,1024]{1,0:T(8,128)(2,1)}, bf16[256,1024]{1,0:T(8,128)(2,1)}, u32[]{:S(2)}, u32[]{:S(2)}) %collective-permute-start.12) | collective-permute-done | bytes 524320 | tf_op jit(solution)/shard_map/ppermute | solution.py:16
  465.7 5.8 %collective-permute-done.11 = bf16[256,1024]{1,0:T(8,128)(2,1)} collective-permute-done((bf16[256,1024]{1,0:T(8,128)(2,1)}, bf16[256,1024]{1,0:T(8,128)(2,1)}, u32[]{:S(2)}, u32[]{:S(2)}) %collective-permute-start.11) | collective-permute-done | bytes 524320 | tf_op jit(solution)/shard_map/ppermute | solution.py:16
  474.5 9.0 %collective-permute-done.10 = bf16[256,1024]{1,0:T(8,128)(2,1)S(1)} collective-permute-done((bf16[256,1024]{1,0:T(8,128)(2,1)S(1)}, bf16[256,1024]{1,0:T(8,128)(2,1)S(1)}, u32[]{:S(2)}, u32[]{:S(2)}) %collective-permute-start.10) | collective-permute-done | bytes 524320 | tf_op jit(solution)/shard_map/ppermute | solution.py:16
  495.8 20.4 %collective-permute-done.16 = bf16[256,1024]{1,0:T(8,128)(2,1)} collective-permute-done((bf16[256,1024]{1,0:T(8,128)(2,1)}, bf16[256,1024]{1,0:T(8,128)(2,1)}, u32[]{:S(2)}, u32[]{:S(2)}) %collective-permute-start.16) | collective-permute-done | bytes 524320 | tf_op jit(solution)/shard_map/ppermute | solution.py:16
  519.0 8.9 %collective-permute-done.15 = bf16[256,1024]{1,0:T(8,128)(2,1)} collective-permute-done((bf16[256,1024]{1,0:T(8,128)(2,1)}, bf16[256,1024]{1,0:T(8,128)(2,1)}, u32[]{:S(2)}, u32[]{:S(2)}) %collective-permute-start.15) | collective-permute-done | bytes 524320 | tf_op jit(solution)/shard_map/ppermute | solution.py:16
  530.6 3.1 add_convert_fusion
  (242 shorter events, 189.8 us)
Async XLA Ops:
  7.2 26.0 %copy-start.30 = (bf16[256,1024]{1,0:T(8,128)(2,1)S(1)}, bf16[256,1024]{1,0:T(8,128)(2,1)}, u32[]{:S(2)}) copy-start(bf16[256,1024]{1,0:T(8,128)(2,1)} %param.6) | copy-start | bytes 1572868
  7.2 303.4 %all-gather.2.cloned.1.call-start = ((), (), s32[]{:S(2)}) async-start(), calls=%async_computation.2 | async-start | bytes 2621440 | tf_op jit(solution)/shard_map/all_gather | solution.py:98
  7.2 157.8 %collective-permute-start = (bf16[256,1024]{1,0:T(8,128)(2,1)}, bf16[256,1024]{1,0:T(8,128)(2,1)}, u32[]{:S(2)}, u32[]{:S(2)}) collective-permute-start(bf16[256,1024]{1,0:T(8,128)(2,1)} %param.7), channel_id=1, source_target_pairs={{0,4},{4,8},{8,12},{12,16},{16,20},{20,24},{24,28},{28,32},{32,36}... | collective-permute-start | bytes 1572872 | tf_op jit(solution)/shard_map/ppermute | solution.py:16
  15.4 174.4 %collective-permute-start.1 = (bf16[256,1024]{1,0:T(8,128)(2,1)}, bf16[256,1024]{1,0:T(8,128)(2,1)}, u32[]{:S(2)}, u32[]{:S(2)}) collective-permute-start(bf16[256,1024]{1,0:T(8,128)(2,1)} %param.7), channel_id=1, source_target_pairs={{0,8},{4,12},{8,16},{12,20},{16,24},{20,28},{24,32},{28,36},{32,40... | collective-permute-start | bytes 1572872 | tf_op jit(solution)/shard_map/ppermute | solution.py:16
  18.6 182.4 %collective-permute-start.2 = (bf16[256,1024]{1,0:T(8,128)(2,1)}, bf16[256,1024]{1,0:T(8,128)(2,1)S(1)}, u32[]{:S(2)}, u32[]{:S(2)}) collective-permute-start(bf16[256,1024]{1,0:T(8,128)(2,1)} %param.7), channel_id=1, source_target_pairs={{0,16},{4,20},{8,24},{12,28},{16,32},{20,36},{24,40},{28,44},{32,4... | collective-permute-start | bytes 1572872 | tf_op jit(solution)/shard_map/ppermute | solution.py:16
  22.6 195.6 %collective-permute-start.3 = (bf16[256,1024]{1,0:T(8,128)(2,1)}, bf16[256,1024]{1,0:T(8,128)(2,1)}, u32[]{:S(2)}, u32[]{:S(2)}) collective-permute-start(bf16[256,1024]{1,0:T(8,128)(2,1)} %param.7), channel_id=1, source_target_pairs={{0,32},{4,36},{8,40},{12,44},{16,48},{20,52},{24,56},{28,60},{32,6... | collective-permute-start | bytes 1572872 | tf_op jit(solution)/shard_map/ppermute | solution.py:16
  25.7 197.8 %collective-permute-start.4 = (bf16[256,1024]{1,0:T(8,128)(2,1)}, bf16[256,1024]{1,0:T(8,128)(2,1)}, u32[]{:S(2)}, u32[]{:S(2)}) collective-permute-start(bf16[256,1024]{1,0:T(8,128)(2,1)} %param.7), channel_id=1, source_target_pairs={{0,64},{4,68},{8,72},{12,76},{16,80},{20,84},{24,88},{28,92},{32,9... | collective-permute-start | bytes 1572872 | tf_op jit(solution)/shard_map/ppermute | solution.py:16
  29.5 505.4 %reduce-scatter.2.cloned.1.call-start = ((), (), s32[]{:S(2)}) async-start(), calls=%async_computation.1 | async-start | bytes 5242880 | tf_op jit(solution)/shard_map/reduce_scatter | solution.py:95
  165.1 71.8 %collective-permute-start.9 = (bf16[256,1024]{1,0:T(8,128)(2,1)}, bf16[256,1024]{1,0:T(8,128)(2,1)}, u32[]{:S(2)}, u32[]{:S(2)}) collective-permute-start(bf16[256,1024]{1,0:T(8,128)(2,1)} %param.8), channel_id=1, source_target_pairs={{0,64},{4,68},{8,72},{12,76},{16,80},{20,84},{24,88},{28,92},{32,9... | collective-permute-start | bytes 1572872 | tf_op jit(solution)/shard_map/ppermute | solution.py:16
  169.3 45.6 %copy-start.16 = (bf16[2,128,1024]{1,2,0:T(8,128)(2,1)}, bf16[2,128,1024]{1,2,0:T(8,128)(2,1)S(1)}, u32[]{:S(2)}) copy-start(bf16[2,128,1024]{1,2,0:T(8,128)(2,1)S(1)} %copy.379) | copy-start | bytes 1572868
  189.8 56.2 %collective-permute-start.8 = (bf16[256,1024]{1,0:T(8,128)(2,1)}, bf16[256,1024]{1,0:T(8,128)(2,1)}, u32[]{:S(2)}, u32[]{:S(2)}) collective-permute-start(bf16[256,1024]{1,0:T(8,128)(2,1)} %param.8), channel_id=1, source_target_pairs={{0,32},{4,36},{8,40},{12,44},{16,48},{20,52},{24,56},{28,60},{32,6... | collective-permute-start | bytes 1572872 | tf_op jit(solution)/shard_map/ppermute | solution.py:16
  201.0 56.2 %collective-permute-start.7 = (bf16[256,1024]{1,0:T(8,128)(2,1)}, bf16[256,1024]{1,0:T(8,128)(2,1)}, u32[]{:S(2)}, u32[]{:S(2)}) collective-permute-start(bf16[256,1024]{1,0:T(8,128)(2,1)} %param.8), channel_id=1, source_target_pairs={{0,16},{4,20},{8,24},{12,28},{16,32},{20,36},{24,40},{28,44},{32,4... | collective-permute-start | bytes 1572872 | tf_op jit(solution)/shard_map/ppermute | solution.py:16
  218.1 45.7 %collective-permute-start.6 = (bf16[256,1024]{1,0:T(8,128)(2,1)}, bf16[256,1024]{1,0:T(8,128)(2,1)}, u32[]{:S(2)}, u32[]{:S(2)}) collective-permute-start(bf16[256,1024]{1,0:T(8,128)(2,1)} %param.8), channel_id=1, source_target_pairs={{0,8},{4,12},{8,16},{12,20},{16,24},{20,28},{24,32},{28,36},{32,40... | collective-permute-start | bytes 1572872 | tf_op jit(solution)/shard_map/ppermute | solution.py:16
  223.5 46.0 %collective-permute-start.5 = (bf16[256,1024]{1,0:T(8,128)(2,1)}, bf16[256,1024]{1,0:T(8,128)(2,1)}, u32[]{:S(2)}, u32[]{:S(2)}) collective-permute-start(bf16[256,1024]{1,0:T(8,128)(2,1)} %param.8), channel_id=1, source_target_pairs={{0,4},{4,8},{8,12},{12,16},{16,20},{20,24},{24,28},{28,32},{32,36}... | collective-permute-start | bytes 1572872 | tf_op jit(solution)/shard_map/ppermute | solution.py:16
  357.4 52.3 %collective-permute-start.14 = (bf16[256,1024]{1,0:T(8,128)(2,1)}, bf16[256,1024]{1,0:T(8,128)(2,1)}, u32[]{:S(2)}, u32[]{:S(2)}) collective-permute-start(bf16[256,1024]{1,0:T(8,128)(2,1)} %bitcast.289), channel_id=1, source_target_pairs={{64,0},{68,4},{72,8},{76,12},{80,16},{84,20},{88,24},{92,28},{96,3... | collective-permute-start | bytes 1572872 | tf_op jit(solution)/shard_map/ppermute | solution.py:16
  366.6 48.0 %collective-permute-start.13 = (bf16[256,1024]{1,0:T(8,128)(2,1)}, bf16[256,1024]{1,0:T(8,128)(2,1)}, u32[]{:S(2)}, u32[]{:S(2)}) collective-permute-start(bf16[256,1024]{1,0:T(8,128)(2,1)} %bitcast.290), channel_id=1, source_target_pairs={{32,0},{36,4},{40,8},{44,12},{48,16},{52,20},{56,24},{60,28},{64,3... | collective-permute-start | bytes 1572872 | tf_op jit(solution)/shard_map/ppermute | solution.py:16
  375.6 87.0 %collective-permute-start.12 = (bf16[256,1024]{1,0:T(8,128)(2,1)}, bf16[256,1024]{1,0:T(8,128)(2,1)}, u32[]{:S(2)}, u32[]{:S(2)}) collective-permute-start(bf16[256,1024]{1,0:T(8,128)(2,1)} %bitcast.291), channel_id=1, source_target_pairs={{16,0},{20,4},{24,8},{28,12},{32,16},{36,20},{40,24},{44,28},{48,3... | collective-permute-start | bytes 1572872 | tf_op jit(solution)/shard_map/ppermute | solution.py:16
  385.5 85.9 %collective-permute-start.11 = (bf16[256,1024]{1,0:T(8,128)(2,1)}, bf16[256,1024]{1,0:T(8,128)(2,1)}, u32[]{:S(2)}, u32[]{:S(2)}) collective-permute-start(bf16[256,1024]{1,0:T(8,128)(2,1)} %bitcast.292), channel_id=1, source_target_pairs={{8,0},{12,4},{16,8},{20,12},{24,16},{28,20},{32,24},{36,28},{40,32... | collective-permute-start | bytes 1572872 | tf_op jit(solution)/shard_map/ppermute | solution.py:16
  392.5 91.0 %collective-permute-start.10 = (bf16[256,1024]{1,0:T(8,128)(2,1)S(1)}, bf16[256,1024]{1,0:T(8,128)(2,1)S(1)}, u32[]{:S(2)}, u32[]{:S(2)}) collective-permute-start(bf16[256,1024]{1,0:T(8,128)(2,1)S(1)} %bitcast.353), channel_id=1, source_target_pairs={{4,0},{8,4},{12,8},{16,12},{20,16},{24,20},{28,24},{32,28},{36,32}... | collective-permute-start | bytes 1572872 | tf_op jit(solution)/shard_map/ppermute | solution.py:16
  409.7 79.6 %collective-permute-start.19 = (bf16[256,1024]{1,0:T(8,128)(2,1)S(1)}, bf16[256,1024]{1,0:T(8,128)(2,1)S(1)}, u32[]{:S(2)}, u32[]{:S(2)}) collective-permute-start(bf16[256,1024]{1,0:T(8,128)(2,1)S(1)} %bitcast.351), channel_id=1, source_target_pairs={{64,0},{68,4},{72,8},{76,12},{80,16},{84,20},{88,24},{92,28},{96,3... | collective-permute-start | bytes 1572872 | tf_op jit(solution)/shard_map/ppermute | solution.py:16
  414.5 76.5 %collective-permute-start.18 = (bf16[256,1024]{1,0:T(8,128)(2,1)}, bf16[256,1024]{1,0:T(8,128)(2,1)S(1)}, u32[]{:S(2)}, u32[]{:S(2)}) collective-permute-start(bf16[256,1024]{1,0:T(8,128)(2,1)} %bitcast.284), channel_id=1, source_target_pairs={{32,0},{36,4},{40,8},{44,12},{48,16},{52,20},{56,24},{60,28},{64,3... | collective-permute-start | bytes 1572872 | tf_op jit(solution)/shard_map/ppermute | solution.py:16
  462.6 30.5 %collective-permute-start.17 = (bf16[256,1024]{1,0:T(8,128)(2,1)}, bf16[256,1024]{1,0:T(8,128)(2,1)}, u32[]{:S(2)}, u32[]{:S(2)}) collective-permute-start(bf16[256,1024]{1,0:T(8,128)(2,1)} %bitcast.285), channel_id=1, source_target_pairs={{16,0},{20,4},{24,8},{28,12},{32,16},{36,20},{40,24},{44,28},{48,3... | collective-permute-start | bytes 1572872 | tf_op jit(solution)/shard_map/ppermute | solution.py:16
  471.5 44.8 %collective-permute-start.16 = (bf16[256,1024]{1,0:T(8,128)(2,1)}, bf16[256,1024]{1,0:T(8,128)(2,1)}, u32[]{:S(2)}, u32[]{:S(2)}) collective-permute-start(bf16[256,1024]{1,0:T(8,128)(2,1)} %bitcast.286), channel_id=1, source_target_pairs={{8,0},{12,4},{16,8},{20,12},{24,16},{28,20},{32,24},{36,28},{40,32... | collective-permute-start | bytes 1572872 | tf_op jit(solution)/shard_map/ppermute | solution.py:16
  483.5 44.4 %collective-permute-start.15 = (bf16[256,1024]{1,0:T(8,128)(2,1)}, bf16[256,1024]{1,0:T(8,128)(2,1)}, u32[]{:S(2)}, u32[]{:S(2)}) collective-permute-start(bf16[256,1024]{1,0:T(8,128)(2,1)} %bitcast.287), channel_id=1, source_target_pairs={{4,0},{8,4},{12,8},{16,12},{20,16},{24,20},{28,24},{32,28},{36,32}... | collective-permute-start | bytes 1572872 | tf_op jit(solution)/shard_map/ppermute | solution.py:16
  (35 other events, 220.2 us)
Sparse Core Ops, SparseCore 0:
  29.6 156.6 all-gather.1
  340.9 83.3 reduce-scatter.1
where the time goes:
time: 553 us; the launch traced here: 544 us
  waiting for transfers between devices  278 us (50%)
  matrix products  86.1 us (16%)
  local copies, waits for them, and re-layouts  72.7 us (13%)
  starting transfers between devices  61.3 us (11%)
  other arithmetic  30.5 us (6%)
  between operations  15.6 us (3%)
    ppermute x20, waiting for transfers between devices, shifted(): lax.ppermute(value, axis, [(source, source + steps) for source in range(i...  277 us
    ppermute x20, starting transfers between devices, shifted(): lax.ppermute(value, axis, [(source, source + steps) for source in range(i...  61.3 us
    unnamed x110, local copies, waits for them, and re-layouts  23.6 us
    dot_general x10, matrix products, pick_blocks(): jnp.einsum('qc,ckd->qkd', chooser(exponent, jnp.bfloat16), fetched.reshap...  22.9 us
    dot_general x6, matrix products, body(): jnp.einsum('bhqk,bqhd->bkhd', portion(probs_low, index), grad_blocks, pre...  13.1 us
    mul x5, local copies, waits for them, and re-layouts, body(): jnp.einsum('bqhd,bkhd->bhqk', query_blocks, distant_keys[exponent], prefe...  11.6 us
    reshape x10, local copies, waits for them, and re-layouts, pick_blocks(): chosen.astype(jnp.bfloat16)  11.5 us
  transfers between devices with their start and end apart: 22, of which 17 were waited for; matrix products, arithmetic and copies ran while one was open for 29% of the time, Pallas kernels for 0%

commit v1 on v0

v1 whole, which is shorter than its diff:
```python
import math

import jax
import jax.numpy as jnp
from jax import lax
from jax.experimental import pallas as pl
from jax.experimental.pallas import tpu as pltpu
from jax.sharding import PartitionSpec as P

HD = 128
BT = 128
LEVELS = 5
SCALE = 1.0 / math.sqrt(HD)
LOG2E = 1.0 / math.log(2.0)
NEG = -1e30
BF = jnp.bfloat16
F32 = jnp.float32
RUNS = 64
GROUPS = 4
NT = (((1,), (1,)), ((), ()))
NN = (((1,), (0,)), ((), ()))
TN = (((0,), (0,)), ((), ()))


def params(mib=48):
    return pltpu.CompilerParams(vmem_limit_bytes=mib * 1024 * 1024)


def dot(a, b, dims):
    return lax.dot_general(a, b, dims, preferred_element_type=F32)


def move(value, target):
    pairs = [(r, target(r)) for r in range(RUNS)]
    return lax.ppermute(value, "seq", [(a, b) for a, b in pairs if b is not None])


def x_of(r):
    return (r >> 3) & 3


def gather_blocks(meta, refs, t, b):
    own = refs[0][t, b * BT : (b + 1) * BT, :]
    far = [refs[1 + j][t, pl.ds(pl.multiple_of(meta[b * LEVELS + j] * BT, BT), BT), :] for j in range(LEVELS)]
    return jnp.concatenate([own] + far, axis=0)


def forward_kernel(meta, q, *refs):
    pairs, (p_out, o_out) = refs[:6], refs[6:]
    position = meta[2 * LEVELS]
    rows = lax.broadcasted_iota(jnp.int32, (BT, BT), 0)
    cols = lax.broadcasted_iota(jnp.int32, (BT, BT), 1)
    for b in range(2):
        mine = slice(b * BT, (b + 1) * BT)
        s = dot(q[mine, :], gather_blocks(meta, pairs, 0, b), NT)
        parts = [jnp.where(rows >= cols, s[:, :BT], NEG)]
        for j in range(LEVELS):
            parts.append(jnp.where(position >= 2**j, s[:, (j + 1) * BT : (j + 2) * BT], NEG))
        s = jnp.concatenate(parts, axis=1)
        peak = jnp.max(s, axis=1, keepdims=True)
        e = jnp.exp2((s - peak) * (SCALE * LOG2E))
        p = (e * (1.0 / jnp.sum(e, axis=1, keepdims=True))).astype(BF)
        p_out[0, mine, :] = p
        o_out[mine, :] = dot(p, gather_blocks(meta, pairs, 1, b), NN).astype(BF)


def forward(meta, queries, pairs):
    heads = queries.shape[1] // HD
    col = pl.BlockSpec((2 * BT, HD), lambda h, m: (0, h))
    both = pl.BlockSpec((2, 2 * BT, HD), lambda h, m: (0, 0, h))
    return pl.pallas_call(
        forward_kernel,
        grid_spec=pltpu.PrefetchScalarGridSpec(
            num_scalar_prefetch=1,
            grid=(heads,),
            in_specs=[col] + [both] * 6,
            out_specs=[pl.BlockSpec((1, 2 * BT, 6 * BT), lambda h, m: (h, 0, 0)), col],
        ),
        out_shape=[
            jax.ShapeDtypeStruct((heads, 2 * BT, 6 * BT), BF),
            jax.ShapeDtypeStruct(queries.shape, BF),
        ],
        compiler_params=params(),
        cost_estimate=pl.CostEstimate(flops=10**9, bytes_accessed=9 * 2**20, transcendentals=10**6),
        name="attend",
    )(meta, queries, *pairs)


def backward_kernel(meta, q, g, o, p_in, *refs):
    pairs, (dq_out, own_out), sends = refs[:6], refs[6:8], refs[8:]
    halves = []
    for b in range(2):
        mine = slice(b * BT, (b + 1) * BT)
        gb = g[mine, :]
        qb = q[mine, :]
        correction = jnp.sum(gb.astype(F32) * o[mine, :].astype(F32), axis=1, keepdims=True)
        p = p_in[0, mine, :]
        dp = dot(gb, gather_blocks(meta, pairs, 1, b), NT)
        ds = (p.astype(F32) * (dp - correction) * SCALE).astype(BF)
        dq_out[mine, :] = dot(ds, gather_blocks(meta, pairs, 0, b), NN).astype(BF)
        dk = dot(ds, qb, TN)
        dv = dot(p, gb, TN)
        own_out[0, mine, :] = dk[:BT]
        own_out[1, mine, :] = dv[:BT]
        halves.append((dk, dv))
    for j in range(LEVELS):
        part = slice((j + 1) * BT, (j + 2) * BT)
        for t in range(2):
            for slot in range(2):
                total = jnp.where(meta[j] == slot, halves[0][t][part], 0.0) + jnp.where(
                    meta[LEVELS + j] == slot, halves[1][t][part], 0.0
                )
                rows = slice(slot * BT, (slot + 1) * BT)
                if j < 3:
                    sends[j][t, rows, :] = total.astype(BF)
                else:
                    sends[3 + 2 * (j - 3) + t][rows, :] = total.astype(BF)


def backward(meta, queries, grads, attended, probs, pairs):
    heads = queries.shape[1] // HD
    col = pl.BlockSpec((2 * BT, HD), lambda h, m: (0, h))
    both = pl.BlockSpec((2, 2 * BT, HD), lambda h, m: (0, 0, h))
    pair = (2,) + queries.shape
    return pl.pallas_call(
        backward_kernel,
        grid_spec=pltpu.PrefetchScalarGridSpec(
            num_scalar_prefetch=1,
            grid=(heads,),
            in_specs=[col] * 3 + [pl.BlockSpec((1, 2 * BT, 6 * BT), lambda h, m: (h, 0, 0))] + [both] * 6,
            out_specs=[col, both] + [both] * 3 + [col] * 4,
        ),
        out_shape=[jax.ShapeDtypeStruct(queries.shape, BF), jax.ShapeDtypeStruct(pair, F32)]
        + [jax.ShapeDtypeStruct(pair, BF)] * 3
        + [jax.ShapeDtypeStruct(queries.shape, BF)] * 4,
        compiler_params=params(),
        cost_estimate=pl.CostEstimate(flops=2 * 10**9, bytes_accessed=19 * 2**20, transcendentals=0),
        name="attend_back",
    )(meta, queries, grads, attended, probs, *pairs)


def project_back_kernel(g, w, out):
    out[...] = dot(g[...], w[...], NT).astype(BF)


def project_back(grads, weight):
    tokens = grads.shape[0]
    tile = 256
    return pl.pallas_call(
        project_back_kernel,
        grid=(weight.shape[0] // tile,),
        in_specs=[
            pl.BlockSpec(grads.shape, lambda i: (0, 0)),
            pl.BlockSpec((tile, weight.shape[1]), lambda i: (i, 0)),
        ],
        out_specs=pl.BlockSpec((tokens, tile), lambda i: (0, i)),
        out_shape=jax.ShapeDtypeStruct((tokens, weight.shape[0]), BF),
        compiler_params=params(),
        cost_estimate=pl.CostEstimate(flops=2 * 10**9, bytes_accessed=10 * 2**20, transcendentals=0),
        name="project_back",
    )(grads, weight)


def project_kernel(a, w, out):
    out[...] = dot(a[...], w[...], NN).astype(BF)


def project(attended, weight):
    tokens, depth = attended.shape
    wide = weight.shape[1] // GROUPS
    tile = 512
    steps = wide // tile
    return pl.pallas_call(
        project_kernel,
        grid=(GROUPS * steps,),
        in_specs=[
            pl.BlockSpec((tokens, depth), lambda i: (0, 0)),
            pl.BlockSpec((depth, tile), lambda i: (0, i)),
        ],
        out_specs=pl.BlockSpec((tokens, tile), lambda i: (i // steps, i % steps)),
        out_shape=jax.ShapeDtypeStruct((GROUPS * tokens, wide), BF),
        compiler_params=params(),
        cost_estimate=pl.CostEstimate(flops=2 * 10**9, bytes_accessed=11 * 2**20, transcendentals=0),
        name="project",
    )(attended, weight)


def nothing(*refs):
    pass


def after(value, *others):
    anywhere = pl.BlockSpec(memory_space=pl.ANY)
    return pl.pallas_call(
        nothing,
        in_specs=[anywhere] * (1 + len(others)),
        out_specs=anywhere,
        out_shape=jax.ShapeDtypeStruct(value.shape, value.dtype),
        input_output_aliases={0: 0},
        cost_estimate=pl.CostEstimate(flops=0, bytes_accessed=0, transcendentals=0),
        name="after",
    )(value, *others)


def body(queries, keys, values, layout, out_weight, out_grad):
    position = lax.axis_index("seq").astype(jnp.int32)
    meta = jnp.concatenate([layout.reshape(-1), position[None]])
    inside = position % 8
    octet = position // 8
    core = position % 2

    pair = jnp.stack([keys, values])
    r16 = move(pair, lambda r: r + 16 if r < 48 else None)
    r8o = move(pair, lambda r: r + 8 if x_of(r) < 3 else None)
    r2o = move(pair, lambda r: r + 2 if r % 8 < 6 else None)
    r4o = move(pair, lambda r: r + 4 if r % 8 < 4 else None)
    r16 = after(r16, r8o, r2o, r4o)
    full_grad = lax.all_gather(after(out_grad, r16), "head", axis=1, tiled=True)
    r8w = move(r16, lambda r: r - 8 if 40 <= r < 48 else None)
    r8 = jnp.where(octet == 4, r8w, r8o)
    r2w = move(r8, lambda r: r - 6 if r % 8 >= 6 else None)
    r4w = move(r8, lambda r: r - 4 if r % 8 >= 4 else None)
    r2 = jnp.where(inside < 2, r2w, r2o)
    r4 = jnp.where(inside < 4, r4w, r4o)
    r1 = move(jnp.where(core == 0, pair, r2), lambda r: r ^ 1)
    pairs = (pair, r1, r2, r4, r8, r16)
    probs, attended = forward(meta, queries, pairs)
    partial = project(attended, out_weight)
    mixed = lax.psum_scatter(partial, "head", scatter_dimension=0, tiled=True)
    grad_attn = project_back(after(full_grad, partial), out_weight)
    dq, own, g1, g2, g4, k8, v8, k16, v16 = backward(meta, queries, grad_attn, attended, probs, pairs)

    crossing = lambda r: r - 16 if 32 <= r < 48 else None
    within = lambda r: r - 16 if x_of(r) >= 2 else None
    near = lambda r: r - 8 if x_of(r) > 0 else None
    s1 = move(g1, lambda r: r ^ 1)
    w4 = move(g4, lambda r: r + 4 if r % 8 < 4 else None)
    xv16 = move(v16, lambda r: r + 16 if 32 <= r < 48 else None)
    zk16 = move(k16, crossing)
    g2 = (g2.astype(F32) + jnp.where(core == 1, s1, 0).astype(F32)).astype(BF)
    w2 = move(g2, lambda r: r + 6 if r % 8 < 2 else None)
    zv16 = move(xv16, lambda r: r - 32 if r >= 48 else None)
    h4 = move(g4, lambda r: r - 4 if r % 8 >= 4 else None)
    h2 = move(g2, lambda r: r - 2 if r % 8 >= 2 else None)
    h16 = [move(k16, within), move(v16, within)]
    w2 = after(w2, *h16)
    k8 = (k8.astype(F32) + w2[0].astype(F32) + w4[0].astype(F32)).astype(BF)
    v8 = (v8.astype(F32) + w2[1].astype(F32) + w4[1].astype(F32)).astype(BF)
    xv8 = move(v8, lambda r: r + 24 if 32 <= r < 40 else None)
    zk8 = move(k8, lambda r: r - 8 if 32 <= r < 40 else None)
    h8 = [move(k8, near), move(v8, near)]
    xv8 = after(xv8, h4, h2, zk16, zv16)
    zv8 = move(xv8, lambda r: r - 32 if r >= 56 else None)
    early = own + jnp.where(core == 0, s1, 0).astype(F32) + h4.astype(F32) + h2.astype(F32)
    totals = []
    for t, terms in ((0, (zk16, h16[0], h8[0], zk8)), (1, (zv16, h16[1], h8[1], zv8))):
        total = early[t]
        for term in terms:
            total = total + term.astype(F32)
        totals.append(total.astype(BF))
    return mixed, dq, totals[0], totals[1]


def solution(mesh):
    placed = (
        P("seq", "head"),
        P("seq", "head"),
        P("seq", "head"),
        P("seq", None),
        P("head", None),
        P("seq", "head"),
    )
    return jax.shard_map(
        body,
        mesh=mesh,
        in_specs=placed,
        out_specs=(P("seq", "head"), P("seq", "head"), P("seq", "head"), P("seq", "head")),
        check_vma=False,
    )
```

time: 553 us -> 305 us (0.55); the launches traced: 544 us -> 303 us
  waiting for transfers between devices: 278 us -> 168 us
  matrix products: 86.1 us -> 0 us
  local copies, waits for them, and re-layouts: 72.7 us -> 8.48 us
  Pallas kernels: 0 us -> 37.6 us
  other arithmetic: 30.5 us -> 17.4 us
    ppermute x20 -> x23, waiting for transfers between devices: 277 us -> 168 us  [move(): lax.ppermute(value, 'seq', [(a, b) for a, b in pairs if b is not None])]
    dot_general x48 -> x0, matrix products: 86.1 us -> none  [the longest x10 22.9 us: pick_blocks(): jnp.einsum('qc,ckd->qkd', chooser(exponent, jnp.bfloat16), fetched.reshap...]
    pallas_call x0 -> x9, Pallas kernels: none -> 37.6 us  [the longest x1 11.8 us: backward(): pl.pallas_call(backward_kernel, grid_spec=pltpu.PrefetchScalarGridSpec(nu...]
    unnamed x110 -> x47, local copies, waits for them, and re-layouts: 23.6 us -> 8.4 us
    reshape x11 -> x1, local copies, waits for them, and re-layouts: 12.9 us -> 0.08 us  [body(): meta = jnp.concatenate([layout.reshape(-1), position[None]])]
    transpose x10 -> x0, local copies, waits for them, and re-layouts: 11.8 us -> none  [the longest x5 8.73 us: body(): jnp.einsum('bhqk,bqhd->bkhd', portion(probs_low, index), grad_blocks, pre...]
    mul x5 -> x0, local copies, waits for them, and re-layouts: 11.6 us -> none  [body(): jnp.einsum('bqhd,bkhd->bhqk', query_blocks, distant_keys[exponent], prefe...]
    convert_element_type x9 -> x0, local copies, waits for them, and re-layouts: 9.17 us -> none  [the longest x5 6.83 us: body(): blocked(back_values).astype(jnp.float32)]
  transfers between devices with their start and end apart: 22 -> 25, of which waited for: 17 -> 12; matrix products, arithmetic and copies ran while one was open for 29% -> 5% of each run, Pallas kernels for 0% -> 12%
where the time goes in v1:
time: 305 us; the launch traced here: 303 us
  waiting for transfers between devices  168 us (55%)
  starting transfers between devices  57.4 us (19%)
  Pallas kernels  37.6 us (12%)
  other arithmetic  17.4 us (6%)
  between operations  14.4 us (5%)
  local copies, waits for them, and re-layouts  8.48 us (3%)
    ppermute x23, waiting for transfers between devices, move(): lax.ppermute(value, 'seq', [(a, b) for a, b in pairs if b is not None])  168 us
    ppermute x23, starting transfers between devices, move(): lax.ppermute(value, 'seq', [(a, b) for a, b in pairs if b is not None])  57.3 us
    pallas_call x1, Pallas kernels, backward(): pl.pallas_call(backward_kernel, grid_spec=pltpu.PrefetchScalarGridSpec(nu...  11.8 us
    pallas_call x1, Pallas kernels, forward(): pl.pallas_call(forward_kernel, grid_spec=pltpu.PrefetchScalarGridSpec(num...  11.5 us
    pallas_call x1, Pallas kernels, project(): pl.pallas_call(project_kernel, grid=(GROUPS * steps,), in_specs=[pl.Block...  8.58 us
    unnamed x47, local copies, waits for them, and re-layouts  8.4 us
  transfers between devices with their start and end apart: 25, of which 12 were waited for; matrix products, arithmetic and copies ran while one was open for 5% of the time, Pallas kernels for 12%

profile of v1, /device:TPU:63, one launch (start us, length us, event | category | flops | bytes accessed | tf_op | source)
XLA Modules:
  0.0 303.3 jit_solution(8420723454349648865)
XLA Ops:
  10.4 8.8 %collective-permute-start = (bf16[2,256,1024]{2,1,0:T(8,128)(2,1)S(1)}, bf16[2,256,1024]{2,1,0:T(8,128)(2,1)S(1)}, u32[]{:S(2)}, u32[]{:S(2)}) collective-permute-start(bf16[2,256,1024]{2,1,0:T(8,128)(2,1)S(1)} %pad_maximum_fusion.refs_0_), channel_id=1, source_target_pairs={{0,64},{4,68},{8,72},{12,76},{16,80},{20,84},{24,88},{28,92},{32,9... | collective-permute-start | bytes 3145736 | tf_op jit(solution)/shard_map/ppermute | solution.py:35
  23.1 40.5 %collective-permute-done.refs_0_ = bf16[2,256,1024]{2,1,0:T(8,128)(2,1)S(1)} collective-permute-done((bf16[2,256,1024]{2,1,0:T(8,128)(2,1)S(1)}, bf16[2,256,1024]{2,1,0:T(8,128)(2,1)S(1)}, u32[]{:S(2)}, u32[]{:S(2)}) %collective-permute-start) | collective-permute-done | bytes 1048608 | tf_op jit(solution)/shard_map/ppermute | solution.py:35
  67.8 5.6 %collective-permute-start.5 = (bf16[2,256,1024]{2,1,0:T(8,128)(2,1)S(1)}, bf16[2,256,1024]{2,1,0:T(8,128)(2,1)}, u32[]{:S(2)}, u32[]{:S(2)}) collective-permute-start(bf16[2,256,1024]{2,1,0:T(8,128)(2,1)S(1)} %broadcast_select_fusion.1.refs_4_), channel_id=1, source_target_pairs={{24,0},{28,4},{56,32},{60,36},{88,64},{92,68},{120,96},{124,100},{... | collective-permute-start | bytes 3145736 | tf_op jit(solution)/shard_map/ppermute | solution.py:35
  75.9 39.7 %collective-permute-done.5 = bf16[2,256,1024]{2,1,0:T(8,128)(2,1)} collective-permute-done((bf16[2,256,1024]{2,1,0:T(8,128)(2,1)S(1)}, bf16[2,256,1024]{2,1,0:T(8,128)(2,1)}, u32[]{:S(2)}, u32[]{:S(2)}) %collective-permute-start.5) | collective-permute-done | bytes 1048608 | tf_op jit(solution)/shard_map/ppermute | solution.py:35
  115.6 2.7 broadcast_select_fusion.3
  118.3 2.7 collective-permute-start.6
  124.7 11.5 %attend.1 = (bf16[8,256,768]{2,1,0:T(8,128)(2,1)}, bf16[256,1024]{1,0:T(8,128)(2,1)S(1)}) custom-call(s32[11]{0:T(128)S(1)} %pad_add_fusion.meta, bf16[256,1024]{1,0:T(8,128)(2,1)S(1)} %copy-done.4, bf16[2,256,1024]{2,1,0:T(8,128)(2,1)S(1)} %pad_maximum_fusion.refs_0_, bf16[2,256,1024]{2,1,0:T(8,128)(2,1)} %collective-permute-done.6.refs_1_, ...), custom_call_target="tpu_custom_call" | custom-call | flops 1000000000 | bytes 9437184 | tf_op jit(solution)/shard_map/attend/pallas_call | solution.py:71
  136.2 8.6 %project.1.refs_1_ = bf16[1024,1024]{1,0:T(8,128)(2,1)} custom-call(bf16[256,1024]{1,0:T(8,128)(2,1)S(1)} %get-tuple-element.15.a.o, bf16[1024,4096]{1,0:T(8,128)(2,1)} %w.3), custom_call_target="tpu_custom_call" | custom-call | flops 2000000000 | bytes 11534336 | tf_op jit(solution)/shard_map/project/pallas_call | solution.py:173
  147.3 5.7 %project_back.1.g = bf16[256,1024]{1,0:T(8,128)(2,1)S(1)} custom-call(bf16[256,4096]{1,0:T(8,128)(2,1)S(1)} %copy-done.3, bf16[1024,4096]{1,0:T(8,128)(2,1)} %w.3), custom_call_target="tpu_custom_call" | custom-call | flops 2000000000 | bytes 10485760 | tf_op jit(solution)/shard_map/project_back/pallas_call | solution.py:149
  153.0 11.8 %attend_back.1 = (bf16[256,1024]{1,0:T(8,128)(2,1)}, f32[2,256,1024]{2,1,0:T(8,128)}, bf16[2,256,1024]{2,1,0:T(8,128)(2,1)S(1)}, bf16[2,256,1024]{2,1,0:T(8,128)...) custom-call(s32[11]{0:T(128)S(1)} %pad_add_fusion.meta, ...), custom_call_target="tpu_custom_call" | custom-call | flops 2000000000 | bytes 19922944 | tf_op jit(solution)/shard_map/attend_back/pallas_call | solution.py:125
  166.0 2.4 collective-permute-done.8
  168.4 2.6 add_convert_fusion
  173.6 3.7 %collective-permute-start.12 = (bf16[256,1024]{1,0:T(8,128)(2,1)}, bf16[256,1024]{1,0:T(8,128)(2,1)S(1)}, u32[]{:S(2)}, u32[]{:S(2)}) collective-permute-start(bf16[256,1024]{1,0:T(8,128)(2,1)} %get-tuple-element.22), channel_id=1, source_target_pairs={{64,0},{68,4},{72,8},{76,12},{80,16},{84,20},{88,24},{92,28},{96,3... | collective-permute-start | bytes 1572872 | tf_op jit(solution)/shard_map/ppermute | solution.py:35
  180.1 9.1 %collective-permute-done.12.refs_1_ = bf16[256,1024]{1,0:T(8,128)(2,1)S(1)} collective-permute-done((bf16[256,1024]{1,0:T(8,128)(2,1)}, bf16[256,1024]{1,0:T(8,128)(2,1)S(1)}, u32[]{:S(2)}, u32[]{:S(2)}) %collective-permute-start.12) | collective-permute-done | bytes 524320 | tf_op jit(solution)/shard_map/ppermute | solution.py:35
  189.2 6.6 %collective-permute-start.9 = (bf16[2,256,1024]{2,1,0:T(8,128)(2,1)}, bf16[2,256,1024]{2,1,0:T(8,128)(2,1)S(1)}, u32[]{:S(2)}, u32[]{:S(2)}) collective-permute-start(bf16[2,256,1024]{2,1,0:T(8,128)(2,1)} %get-tuple-element.20), channel_id=1, source_target_pairs={{16,0},{20,4},{24,8},{28,12},{48,32},{52,36},{56,40},{60,44},{80,6... | collective-permute-start | bytes 3145736 | tf_op jit(solution)/shard_map/ppermute | solution.py:35
  195.8 4.2 %collective-permute-done.14.refs_2_ = bf16[256,1024]{1,0:T(8,128)(2,1)S(1)} collective-permute-done((bf16[256,1024]{1,0:T(8,128)(2,1)S(1)}, bf16[256,1024]{1,0:T(8,128)(2,1)S(1)}, u32[]{:S(2)}, u32[]{:S(2)}) %collective-permute-start.14) | collective-permute-done | bytes 524320 | tf_op jit(solution)/shard_map/ppermute | solution.py:35
  203.6 17.7 %collective-permute-done.13.refs_0_ = bf16[2,256,1024]{2,1,0:T(8,128)(2,1)S(1)} collective-permute-done((bf16[2,256,1024]{2,1,0:T(8,128)(2,1)}, bf16[2,256,1024]{2,1,0:T(8,128)(2,1)S(1)}, u32[]{:S(2)}, u32[]{:S(2)}) %collective-permute-start.13) | collective-permute-done | bytes 1048608 | tf_op jit(solution)/shard_map/ppermute | solution.py:35
  222.6 3.2 %fusion.10 = (bf16[256,1024]{1,0:T(8,128)(2,1)}, bf16[256,1024]{1,0:T(8,128)(2,1)}) fusion(bf16[256,1024]{1,0:T(8,128)(2,1)S(1)} %get-tuple-element.25, bf16[2,256,1024]{2,1,0:T(8,128)(2,1)} %collective-permute-done.15, bf16[2,256,1024]{2,1,0:T(8,128)(2,1)} %after.8, bf16[256,1024]{1,0:T(8,128)(2,1)S(1)} %get-tuple-element.23), kind=kLoop, calls=%fused_computation.16 | loop fusion | flops 3145728 | bytes 4194304 | tf_op jit(solution)/shard_map/convert_element_type | solution.py:248
  227.3 27.9 %collective-permute-done.11.refs_3_ = bf16[256,1024]{1,0:T(8,128)(2,1)} collective-permute-done((bf16[256,1024]{1,0:T(8,128)(2,1)}, bf16[256,1024]{1,0:T(8,128)(2,1)}, u32[]{:S(2)}, u32[]{:S(2)}) %collective-permute-start.11) | collective-permute-done | bytes 524320 | tf_op jit(solution)/shard_map/ppermute | solution.py:35
  255.1 5.0 %collective-permute-start.20 = (bf16[256,1024]{1,0:T(8,128)(2,1)}, bf16[256,1024]{1,0:T(8,128)(2,1)}, u32[]{:S(2)}, u32[]{:S(2)}) collective-permute-start(bf16[256,1024]{1,0:T(8,128)(2,1)} %get-tuple-element.30), channel_id=1, source_target_pairs={{32,0},{36,4},{40,8},{44,12},{48,16},{52,20},{56,24},{60,28},{64,3... | collective-permute-start | bytes 1572872 | tf_op jit(solution)/shard_map/ppermute | solution.py:35
  267.4 3.1 %collective-permute-done.20 = bf16[256,1024]{1,0:T(8,128)(2,1)} collective-permute-done((bf16[256,1024]{1,0:T(8,128)(2,1)}, bf16[256,1024]{1,0:T(8,128)(2,1)}, u32[]{:S(2)}, u32[]{:S(2)}) %collective-permute-start.20) | collective-permute-done | bytes 524320 | tf_op jit(solution)/shard_map/ppermute | solution.py:35
  270.5 10.8 %collective-permute-done.17 = bf16[256,1024]{1,0:T(8,128)(2,1)} collective-permute-done((bf16[256,1024]{1,0:T(8,128)(2,1)}, bf16[256,1024]{1,0:T(8,128)(2,1)}, u32[]{:S(2)}, u32[]{:S(2)}) %collective-permute-start.17) | collective-permute-done | bytes 524320 | tf_op jit(solution)/shard_map/ppermute | solution.py:35
  281.7 11.1 %collective-permute-done.22 = bf16[256,1024]{1,0:T(8,128)(2,1)S(1)} collective-permute-done((bf16[256,1024]{1,0:T(8,128)(2,1)}, bf16[256,1024]{1,0:T(8,128)(2,1)S(1)}, u32[]{:S(2)}, u32[]{:S(2)}) %collective-permute-start.22) | collective-permute-done | bytes 524320 | tf_op jit(solution)/shard_map/ppermute | solution.py:35
  292.8 3.7 %fusion.4 = (bf16[256,1024]{1,0:T(8,128)(2,1)}, bf16[256,1024]{1,0:T(8,128)(2,1)}) fusion(f32[2,256,1024]{2,1,0:T(8,128)S(1)} %convert_add_fusion, bf16[256,1024]{1,0:T(8,128)(2,1)S(1)} %collective-permute-done.22, bf16[256,1024]{1,0:T(8,128)(2,1)} %collective-permute-done.20, bf16[256,1024]{1,0:T(8,128)(2,1)S(1)} %copy-done.20, ...), kind=kLoop, calls=%fused_computation.7 | loop fusion | flops 4718592 | bytes 7340032 | tf_op jit(solution)/shard_map/convert_element_type | solution.py:260
  (94 shorter events, 40.3 us)
Async XLA Ops:
  7.2 138.5 %all-gather.2.cloned.1.call-start = ((), (), s32[]{:S(2)}) async-start(), calls=%async_computation.2 | async-start | bytes 2621440 | tf_op jit(solution)/shard_map/all_gather | solution.py:218
  10.4 53.2 %collective-permute-start = (bf16[2,256,1024]{2,1,0:T(8,128)(2,1)S(1)}, bf16[2,256,1024]{2,1,0:T(8,128)(2,1)S(1)}, u32[]{:S(2)}, u32[]{:S(2)}) collective-permute-start(bf16[2,256,1024]{2,1,0:T(8,128)(2,1)S(1)} %pad_maximum_fusion.refs_0_), channel_id=1, source_target_pairs={{0,64},{4,68},{8,72},{12,76},{16,80},{20,84},{24,88},{28,92},{32,9... | collective-permute-start | bytes 3145736 | tf_op jit(solution)/shard_map/ppermute | solution.py:35
  19.2 44.4 %collective-permute-start.1 = (bf16[2,256,1024]{2,1,0:T(8,128)(2,1)S(1)}, bf16[2,256,1024]{2,1,0:T(8,128)(2,1)S(1)}, u32[]{:S(2)}, u32[]{:S(2)}) collective-permute-start(bf16[2,256,1024]{2,1,0:T(8,128)(2,1)S(1)} %pad_maximum_fusion.refs_0_), channel_id=1, source_target_pairs={{0,32},{4,36},{8,40},{12,44},{16,48},{20,52},{24,56},{28,60},{32,6... | collective-permute-start | bytes 3145736 | tf_op jit(solution)/shard_map/ppermute | solution.py:35
  20.5 43.1 %collective-permute-start.2 = (bf16[2,256,1024]{2,1,0:T(8,128)(2,1)S(1)}, bf16[2,256,1024]{2,1,0:T(8,128)(2,1)}, u32[]{:S(2)}, u32[]{:S(2)}) collective-permute-start(bf16[2,256,1024]{2,1,0:T(8,128)(2,1)S(1)} %pad_maximum_fusion.refs_0_), channel_id=1, source_target_pairs={{0,8},{4,12},{8,16},{12,20},{16,24},{20,28},{32,40},{36,44},{40,48... | collective-permute-start | bytes 3145736 | tf_op jit(solution)/shard_map/ppermute | solution.py:35
  21.8 42.8 %collective-permute-start.3 = (bf16[2,256,1024]{2,1,0:T(8,128)(2,1)S(1)}, bf16[2,256,1024]{2,1,0:T(8,128)(2,1)S(1)}, u32[]{:S(2)}, u32[]{:S(2)}) collective-permute-start(bf16[2,256,1024]{2,1,0:T(8,128)(2,1)S(1)} %pad_maximum_fusion.refs_0_), channel_id=1, source_target_pairs={{0,16},{4,20},{8,24},{12,28},{32,48},{36,52},{40,56},{44,60},{64,8... | collective-permute-start | bytes 3145736 | tf_op jit(solution)/shard_map/ppermute | solution.py:35
  67.6 228.9 %reduce-scatter.2.cloned.1.call-start = ((), (), s32[]{:S(2)}) async-start(), calls=%async_computation.1 | async-start | bytes 2621440 | tf_op jit(solution)/shard_map/reduce_scatter | solution.py:229
  67.8 47.7 %collective-permute-start.5 = (bf16[2,256,1024]{2,1,0:T(8,128)(2,1)S(1)}, bf16[2,256,1024]{2,1,0:T(8,128)(2,1)}, u32[]{:S(2)}, u32[]{:S(2)}) collective-permute-start(bf16[2,256,1024]{2,1,0:T(8,128)(2,1)S(1)} %broadcast_select_fusion.1.refs_4_), channel_id=1, source_target_pairs={{24,0},{28,4},{56,32},{60,36},{88,64},{92,68},{120,96},{124,100},{... | collective-permute-start | bytes 3145736 | tf_op jit(solution)/shard_map/ppermute | solution.py:35
  73.5 47.7 %collective-permute-start.7 = (bf16[2,256,1024]{2,1,0:T(8,128)(2,1)S(1)}, bf16[2,256,1024]{2,1,0:T(8,128)(2,1)}, u32[]{:S(2)}, u32[]{:S(2)}) collective-permute-start(bf16[2,256,1024]{2,1,0:T(8,128)(2,1)S(1)} %broadcast_select_fusion.1.refs_4_), channel_id=1, source_target_pairs={{16,0},{20,4},{24,8},{28,12},{48,32},{52,36},{56,40},{60,44},{80,6... | collective-permute-start | bytes 3145736 | tf_op jit(solution)/shard_map/ppermute | solution.py:35
  118.3 5.4 %collective-permute-start.6 = (bf16[2,256,1024]{2,1,0:T(8,128)(2,1)}, bf16[2,256,1024]{2,1,0:T(8,128)(2,1)}, u32[]{:S(2)}, u32[]{:S(2)}) collective-permute-start(bf16[2,256,1024]{2,1,0:T(8,128)(2,1)} %get-tuple-element.26), channel_id=1, source_target_pairs={{0,4},{4,0},{8,12},{12,8},{16,20},{20,16},{24,28},{28,24},{32,36},... | collective-permute-start | bytes 3145736 | tf_op jit(solution)/shard_map/ppermute | solution.py:35
  165.6 2.8 collective-permute-start.8
  171.0 50.3 %collective-permute-start.13 = (bf16[2,256,1024]{2,1,0:T(8,128)(2,1)}, bf16[2,256,1024]{2,1,0:T(8,128)(2,1)S(1)}, u32[]{:S(2)}, u32[]{:S(2)}) collective-permute-start(bf16[2,256,1024]{2,1,0:T(8,128)(2,1)} %add_convert_fusion), channel_id=1, source_target_pairs={{0,24},{4,28},{32,56},{36,60},{64,88},{68,92},{96,120},{100,124},{... | collective-permute-start | bytes 3145736 | tf_op jit(solution)/shard_map/ppermute | solution.py:35
  172.3 50.3 %collective-permute-start.15 = (bf16[2,256,1024]{2,1,0:T(8,128)(2,1)}, bf16[2,256,1024]{2,1,0:T(8,128)(2,1)}, u32[]{:S(2)}, u32[]{:S(2)}) collective-permute-start(bf16[2,256,1024]{2,1,0:T(8,128)(2,1)} %get-tuple-element.20), channel_id=1, source_target_pairs={{0,16},{4,20},{8,24},{12,28},{32,48},{36,52},{40,56},{44,60},{64,8... | collective-permute-start | bytes 3145736 | tf_op jit(solution)/shard_map/ppermute | solution.py:35
  173.6 15.6 %collective-permute-start.12 = (bf16[256,1024]{1,0:T(8,128)(2,1)}, bf16[256,1024]{1,0:T(8,128)(2,1)S(1)}, u32[]{:S(2)}, u32[]{:S(2)}) collective-permute-start(bf16[256,1024]{1,0:T(8,128)(2,1)} %get-tuple-element.22), channel_id=1, source_target_pairs={{64,0},{68,4},{72,8},{76,12},{80,16},{84,20},{88,24},{92,28},{96,3... | collective-permute-start | bytes 1572872 | tf_op jit(solution)/shard_map/ppermute | solution.py:35
  177.3 22.7 %collective-permute-start.14 = (bf16[256,1024]{1,0:T(8,128)(2,1)S(1)}, bf16[256,1024]{1,0:T(8,128)(2,1)S(1)}, u32[]{:S(2)}, u32[]{:S(2)}) collective-permute-start(bf16[256,1024]{1,0:T(8,128)(2,1)S(1)} %copy-done.9), channel_id=1, source_target_pairs={{64,0},{68,4},{72,8},{76,12},{80,16},{84,20},{88,24},{92,28},{96,3... | collective-permute-start | bytes 1572872 | tf_op jit(solution)/shard_map/ppermute | solution.py:35
  178.6 23.7 %collective-permute-start.18 = (bf16[256,1024]{1,0:T(8,128)(2,1)S(1)}, bf16[256,1024]{1,0:T(8,128)(2,1)}, u32[]{:S(2)}, u32[]{:S(2)}) collective-permute-start(bf16[256,1024]{1,0:T(8,128)(2,1)S(1)} %copy-done.9), channel_id=1, source_target_pairs={{128,192},{132,196},{136,200},{140,204},{144,208},{148,212},{152,2... | collective-permute-start | bytes 1572872 | tf_op jit(solution)/shard_map/ppermute | solution.py:35
  189.2 72.4 %collective-permute-start.9 = (bf16[2,256,1024]{2,1,0:T(8,128)(2,1)}, bf16[2,256,1024]{2,1,0:T(8,128)(2,1)S(1)}, u32[]{:S(2)}, u32[]{:S(2)}) collective-permute-start(bf16[2,256,1024]{2,1,0:T(8,128)(2,1)} %get-tuple-element.20), channel_id=1, source_target_pairs={{16,0},{20,4},{24,8},{28,12},{48,32},{52,36},{56,40},{60,44},{80,6... | collective-permute-start | bytes 3145736 | tf_op jit(solution)/shard_map/ppermute | solution.py:35
  200.0 63.7 %collective-permute-start.10 = (bf16[2,256,1024]{2,1,0:T(8,128)(2,1)}, bf16[2,256,1024]{2,1,0:T(8,128)(2,1)}, u32[]{:S(2)}, u32[]{:S(2)}) collective-permute-start(bf16[2,256,1024]{2,1,0:T(8,128)(2,1)} %add_convert_fusion), channel_id=1, source_target_pairs={{8,0},{12,4},{16,8},{20,12},{24,16},{28,20},{40,32},{44,36},{48,40... | collective-permute-start | bytes 3145736 | tf_op jit(solution)/shard_map/ppermute | solution.py:35
  202.3 52.8 %collective-permute-start.11 = (bf16[256,1024]{1,0:T(8,128)(2,1)}, bf16[256,1024]{1,0:T(8,128)(2,1)}, u32[]{:S(2)}, u32[]{:S(2)}) collective-permute-start(bf16[256,1024]{1,0:T(8,128)(2,1)} %get-tuple-element.22), channel_id=1, source_target_pairs={{128,64},{132,68},{136,72},{140,76},{144,80},{148,84},{152,88},{15... | collective-permute-start | bytes 1572872 | tf_op jit(solution)/shard_map/ppermute | solution.py:35
  221.3 38.9 %collective-permute-start.19 = (bf16[256,1024]{1,0:T(8,128)(2,1)}, bf16[256,1024]{1,0:T(8,128)(2,1)}, u32[]{:S(2)}, u32[]{:S(2)}) collective-permute-start(bf16[256,1024]{1,0:T(8,128)(2,1)} %collective-permute-done.18), channel_id=1, source_target_pairs={{192,64},{196,68},{200,72},{204,76},{208,80},{212,84},{216,88},{22... | collective-permute-start | bytes 1572872 | tf_op jit(solution)/shard_map/ppermute | solution.py:35
  225.8 37.9 %collective-permute-start.21 = (bf16[256,1024]{1,0:T(8,128)(2,1)}, bf16[256,1024]{1,0:T(8,128)(2,1)}, u32[]{:S(2)}, u32[]{:S(2)}) collective-permute-start(bf16[256,1024]{1,0:T(8,128)(2,1)} %get-tuple-element.30), channel_id=1, source_target_pairs={{128,224},{132,228},{136,232},{140,236},{144,240},{148,244},{152,2... | collective-permute-start | bytes 1572872 | tf_op jit(solution)/shard_map/ppermute | solution.py:35
  255.1 15.3 %collective-permute-start.20 = (bf16[256,1024]{1,0:T(8,128)(2,1)}, bf16[256,1024]{1,0:T(8,128)(2,1)}, u32[]{:S(2)}, u32[]{:S(2)}) collective-permute-start(bf16[256,1024]{1,0:T(8,128)(2,1)} %get-tuple-element.30), channel_id=1, source_target_pairs={{32,0},{36,4},{40,8},{44,12},{48,16},{52,20},{56,24},{60,28},{64,3... | collective-permute-start | bytes 1572872 | tf_op jit(solution)/shard_map/ppermute | solution.py:35
  260.2 21.1 %collective-permute-start.17 = (bf16[256,1024]{1,0:T(8,128)(2,1)}, bf16[256,1024]{1,0:T(8,128)(2,1)}, u32[]{:S(2)}, u32[]{:S(2)}) collective-permute-start(bf16[256,1024]{1,0:T(8,128)(2,1)} %get-tuple-element.31), channel_id=1, source_target_pairs={{128,96},{132,100},{136,104},{140,108},{144,112},{148,116},{152,12... | collective-permute-start | bytes 1572872 | tf_op jit(solution)/shard_map/ppermute | solution.py:35
  261.6 20.1 %collective-permute-start.16 = (bf16[256,1024]{1,0:T(8,128)(2,1)}, bf16[256,1024]{1,0:T(8,128)(2,1)}, u32[]{:S(2)}, u32[]{:S(2)}) collective-permute-start(bf16[256,1024]{1,0:T(8,128)(2,1)} %get-tuple-element.31), channel_id=1, source_target_pairs={{32,0},{36,4},{40,8},{44,12},{48,16},{52,20},{56,24},{60,28},{64,3... | collective-permute-start | bytes 1572872 | tf_op jit(solution)/shard_map/ppermute | solution.py:35
  263.7 29.0 %collective-permute-start.22 = (bf16[256,1024]{1,0:T(8,128)(2,1)}, bf16[256,1024]{1,0:T(8,128)(2,1)S(1)}, u32[]{:S(2)}, u32[]{:S(2)}) collective-permute-start(bf16[256,1024]{1,0:T(8,128)(2,1)} %after.9), channel_id=1, source_target_pairs={{224,96},{228,100},{232,104},{236,108},{240,112},{244,116},{248,12... | collective-permute-start | bytes 1572872 | tf_op jit(solution)/shard_map/ppermute | solution.py:35
  (24 other events, 394.0 us)
Sparse Core Ops, SparseCore 0:
  67.7 52.6 all-gather.1
  145.8 70.3 reduce-scatter.1

commit v2 on v1

v2 whole, which is shorter than its diff:
```python
import math

import jax
import jax.numpy as jnp
from jax import lax
from jax.experimental import pallas as pl
from jax.experimental.pallas import tpu as pltpu
from jax.sharding import PartitionSpec as P

HD = 128
BT = 128
LEVELS = 5
SCALE = 1.0 / math.sqrt(HD)
LOG2E = 1.0 / math.log(2.0)
NEG = -1e30
BF = jnp.bfloat16
F32 = jnp.float32
RUNS = 64
GROUPS = 4
STEP = 2
NT = (((1,), (1,)), ((), ()))
NN = (((1,), (0,)), ((), ()))
TN = (((0,), (0,)), ((), ()))


def params(mib=48):
    return pltpu.CompilerParams(vmem_limit_bytes=mib * 1024 * 1024)


def dot(a, b, dims):
    return lax.dot_general(a, b, dims, preferred_element_type=F32)


def move(value, target):
    pairs = [(r, target(r)) for r in range(RUNS)]
    return lax.ppermute(value, "seq", [(a, b) for a, b in pairs if b is not None])


def x_of(r):
    return (r >> 3) & 3


KEY_REFS = (1, 1, 2, 2, 1, 1)
VALUE_REFS = (1, 1, 2, 2, 1, 2)


def grouped(refs, counts):
    groups, at = [], 0
    for count in counts:
        groups.append(refs[at : at + count])
        at += count
    return groups


def gather_blocks(meta, groups, b, cols):
    blocks = [groups[0][0][b * BT : (b + 1) * BT, cols]]
    for j in range(LEVELS):
        rows = pl.ds(pl.multiple_of(meta[b * LEVELS + j] * BT, BT), BT)
        block = groups[1 + j][0][rows, cols]
        if len(groups[1 + j]) == 2:
            block = block + groups[1 + j][1][rows, cols]
        blocks.append(block)
    return jnp.concatenate(blocks, axis=0)


def forward_kernel(meta, q, *refs):
    keys, values = grouped(refs[:8], KEY_REFS), grouped(refs[8:17], VALUE_REFS)
    p_out, o_out = refs[17:]
    position = meta[2 * LEVELS]
    rows = lax.broadcasted_iota(jnp.int32, (BT, BT), 0)
    cols = lax.broadcasted_iota(jnp.int32, (BT, BT), 1)
    for h, b in [(h, b) for h in range(STEP) for b in range(2)]:
        mine = slice(b * BT, (b + 1) * BT)
        here = slice(h * HD, (h + 1) * HD)
        s = dot(q[mine, here], gather_blocks(meta, keys, b, here), NT)
        parts = [jnp.where(rows >= cols, s[:, :BT], NEG)]
        for j in range(LEVELS):
            parts.append(jnp.where(position >= 2**j, s[:, (j + 1) * BT : (j + 2) * BT], NEG))
        s = jnp.concatenate(parts, axis=1)
        peak = jnp.max(s, axis=1, keepdims=True)
        e = jnp.exp2((s - peak) * (SCALE * LOG2E))
        p = (e * (1.0 / jnp.sum(e, axis=1, keepdims=True))).astype(BF)
        p_out[h, mine, :] = p
        o_out[mine, here] = dot(p, gather_blocks(meta, values, b, here), NN).astype(BF)


def forward(meta, queries, keys, values):
    heads = queries.shape[1] // HD
    col = pl.BlockSpec((2 * BT, STEP * HD), lambda h, m: (0, h))
    return pl.pallas_call(
        forward_kernel,
        grid_spec=pltpu.PrefetchScalarGridSpec(
            num_scalar_prefetch=1,
            grid=(heads // STEP,),
            in_specs=[col] * 18,
            out_specs=[pl.BlockSpec((STEP, 2 * BT, 6 * BT), lambda h, m: (h, 0, 0)), col],
        ),
        out_shape=[
            jax.ShapeDtypeStruct((heads, 2 * BT, 6 * BT), BF),
            jax.ShapeDtypeStruct(queries.shape, BF),
        ],
        compiler_params=params(),
        cost_estimate=pl.CostEstimate(flops=10**9, bytes_accessed=9 * 2**20, transcendentals=10**6),
        name="attend",
    )(meta, queries, *keys, *values)


def backward_kernel(meta, q, g, o, p_in, *refs):
    keys, values = grouped(refs[:8], KEY_REFS), grouped(refs[8:17], VALUE_REFS)
    (dq_out, own_out), sends = refs[17:19], refs[19:]
    for h in range(STEP):
        here = slice(h * HD, (h + 1) * HD)
        halves = []
        for b in range(2):
            mine = slice(b * BT, (b + 1) * BT)
            gb = g[mine, here]
            qb = q[mine, here]
            correction = jnp.sum(gb.astype(F32) * o[mine, here].astype(F32), axis=1, keepdims=True)
            p = p_in[h, mine, :]
            dp = dot(gb, gather_blocks(meta, values, b, here), NT)
            ds = (p.astype(F32) * (dp - correction) * SCALE).astype(BF)
            dq_out[mine, here] = dot(ds, gather_blocks(meta, keys, b, here), NN).astype(BF)
            dk = dot(ds, qb, TN)
            dv = dot(p, gb, TN)
            own_out[0, mine, here] = dk[:BT]
            own_out[1, mine, here] = dv[:BT]
            halves.append((dk, dv))
        for j in range(LEVELS):
            part = slice((j + 1) * BT, (j + 2) * BT)
            for t in range(2):
                for slot in range(2):
                    total = jnp.where(meta[j] == slot, halves[0][t][part], 0.0) + jnp.where(
                        meta[LEVELS + j] == slot, halves[1][t][part], 0.0
                    )
                    rows = slice(slot * BT, (slot + 1) * BT)
                    if j < 3:
                        sends[j][t, rows, here] = total.astype(BF)
                    else:
                        sends[3 + 2 * (j - 3) + t][rows, here] = total.astype(BF)


def backward(meta, queries, grads, attended, probs, keys, values):
    heads = queries.shape[1] // HD
    col = pl.BlockSpec((2 * BT, STEP * HD), lambda h, m: (0, h))
    both = pl.BlockSpec((2, 2 * BT, STEP * HD), lambda h, m: (0, 0, h))
    pair = (2,) + queries.shape
    return pl.pallas_call(
        backward_kernel,
        grid_spec=pltpu.PrefetchScalarGridSpec(
            num_scalar_prefetch=1,
            grid=(heads // STEP,),
            in_specs=[col] * 3
            + [pl.BlockSpec((STEP, 2 * BT, 6 * BT), lambda h, m: (h, 0, 0))]
            + [col] * 17,
            out_specs=[col, both] + [both] * 3 + [col] * 4,
        ),
        out_shape=[pltpu.HBM(queries.shape, BF), pltpu.HBM(pair, F32)]
        + [pltpu.HBM(pair, BF)] * 3
        + [pltpu.HBM(queries.shape, BF)] * 4,
        compiler_params=params(),
        cost_estimate=pl.CostEstimate(flops=2 * 10**9, bytes_accessed=19 * 2**20, transcendentals=0),
        name="attend_back",
    )(meta, queries, grads, attended, probs, *keys, *values)


def project_back_kernel(g, w, out):
    out[...] = dot(g[...], w[...], NT).astype(BF)


def project_back(grads, weight):
    tokens = grads.shape[0]
    tile = 256
    return pl.pallas_call(
        project_back_kernel,
        grid=(weight.shape[0] // tile,),
        in_specs=[
            pl.BlockSpec(grads.shape, lambda i: (0, 0)),
            pl.BlockSpec((tile, weight.shape[1]), lambda i: (i, 0)),
        ],
        out_specs=pl.BlockSpec((tokens, tile), lambda i: (0, i)),
        out_shape=jax.ShapeDtypeStruct((tokens, weight.shape[0]), BF),
        compiler_params=params(),
        cost_estimate=pl.CostEstimate(flops=2 * 10**9, bytes_accessed=10 * 2**20, transcendentals=0),
        name="project_back",
    )(grads, weight)


def project_kernel(a, w, out):
    out[...] = dot(a[...], w[...], NN).astype(BF)


def project(attended, weight):
    tokens, depth = attended.shape
    wide = weight.shape[1] // GROUPS
    tile = 512
    steps = wide // tile
    return pl.pallas_call(
        project_kernel,
        grid=(GROUPS * steps,),
        in_specs=[
            pl.BlockSpec((tokens, depth), lambda i: (0, 0)),
            pl.BlockSpec((depth, tile), lambda i: (0, i)),
        ],
        out_specs=pl.BlockSpec((tokens, tile), lambda i: (i // steps, i % steps)),
        out_shape=jax.ShapeDtypeStruct((GROUPS * tokens, wide), BF),
        compiler_params=params(),
        cost_estimate=pl.CostEstimate(flops=2 * 10**9, bytes_accessed=11 * 2**20, transcendentals=0),
        name="project",
    )(attended, weight)


def nothing(*refs):
    pass


def after(value, *others, flops=0):
    anywhere = pl.BlockSpec(memory_space=pl.ANY)
    return pl.pallas_call(
        nothing,
        in_specs=[anywhere] * (1 + len(others)),
        out_specs=anywhere,
        out_shape=jax.ShapeDtypeStruct(value.shape, value.dtype),
        input_output_aliases={0: 0},
        cost_estimate=pl.CostEstimate(flops=flops, bytes_accessed=0, transcendentals=0),
        name="after",
    )(value, *others)


def body(queries, keys, values, layout, out_weight, out_grad):
    position = lax.axis_index("seq").astype(jnp.int32)
    meta = jnp.concatenate([layout.reshape(-1), position[None]])
    octet = position // 8
    core = position % 2

    def roots(own):
        return (
            move(own, lambda r: r + 8 if x_of(r) < 3 else None),
            move(own, lambda r: r + 2 if r % 8 < 6 else None),
            move(own, lambda r: r + 4 if r % 8 < 4 else None),
        )

    def wraps(own, r8o, r2o, r4o, crossed, *others, flops=0):
        r8w = move(crossed, lambda r: r - 8 if 40 <= r < 48 else None)
        r8 = jnp.where(octet == 4, r8w, r8o)
        r2w = move(r8, lambda r: r - 6 if r % 8 >= 6 else None)
        r4w = move(r8, lambda r: r - 4 if r % 8 >= 4 else None)
        r1 = after(jnp.where(core == 0, own, r2o + r2w), r4w, *others, flops=flops)
        return move(r1, lambda r: r ^ 1), r2o, r2w, r4o, r4w, r8

    k16 = move(keys, lambda r: r + 16 if r < 48 else None)
    v16a = move(values, lambda r: (r & 32) | ((r + 16) & 31) if r < 48 else None)
    k_roots = roots(keys)
    v_roots = roots(values)
    v16z = after(move(v16a, lambda r: r + 32 if r < 16 else None), flops=10**10)
    k16 = after(k16, *k_roots)
    key_set = (keys,) + wraps(keys, *k_roots, k16, flops=10**10) + (k16,)
    full_grad = lax.all_gather(after(out_grad, v16z, key_set[6]), "head", axis=1, tiled=True)
    value_set = (values,) + wraps(values, *v_roots, v16z, key_set[1]) + (v16a, v16z)
    probs, attended = forward(meta, queries, key_set, value_set)
    grad_attn = project_back(after(full_grad, attended), out_weight)
    dq, own, g1, g2, g4, k8, v8, k16, v16 = backward(
        meta, queries, grad_attn, attended, probs, key_set, value_set
    )
    crossing = lambda r: r - 16 if 32 <= r < 48 else None
    within = lambda r: r - 16 if x_of(r) >= 2 else None
    near = lambda r: r - 8 if x_of(r) > 0 else None
    s1 = move(g1, lambda r: r ^ 1)
    w4 = move(g4, lambda r: r + 4 if r % 8 < 4 else None)
    xv16 = move(v16, lambda r: r + 16 if 32 <= r < 48 else None)
    zk16 = move(k16, crossing)
    g2 = g2 + jnp.where(core == 1, s1, 0)
    w2 = move(g2, lambda r: r + 6 if r % 8 < 2 else None)
    partial = project(after(attended, g2), out_weight)
    mixed = lax.psum_scatter(partial, "head", scatter_dimension=0, tiled=True)
    zv16 = move(xv16, lambda r: r - 32 if r >= 48 else None)
    h4 = move(g4, lambda r: r - 4 if r % 8 >= 4 else None)
    h2 = move(g2, lambda r: r - 2 if r % 8 >= 2 else None)
    h16 = [move(k16, within), move(v16, within)]
    w2 = after(w2, w4, zk16, zv16, flops=4 * 10**10)
    k8 = (k8.astype(F32) + w2[0].astype(F32) + w4[0].astype(F32)).astype(BF)
    v8 = (v8.astype(F32) + w2[1].astype(F32) + w4[1].astype(F32)).astype(BF)
    xv8 = move(v8, lambda r: r + 24 if 32 <= r < 40 else None)
    zk8 = move(k8, lambda r: r - 8 if 32 <= r < 40 else None)
    h8 = [move(k8, near), move(v8, near)]
    xv8 = after(xv8, h4, *h16)
    zv8 = move(xv8, lambda r: r - 32 if r >= 56 else None)
    early = own + jnp.where(core == 0, s1, 0).astype(F32) + h4.astype(F32) + h2.astype(F32)
    totals = []
    for t, terms in ((0, (zk16, h16[0], h8[0], zk8)), (1, (zv16, h16[1], h8[1], zv8))):
        total = early[t]
        for term in terms:
            total = total + term.astype(F32)
        totals.append(total.astype(BF))
    return mixed, dq, totals[0], totals[1]


def solution(mesh):
    placed = (
        P("seq", "head"),
        P("seq", "head"),
        P("seq", "head"),
        P("seq", None),
        P("head", None),
        P("seq", "head"),
    )
    return jax.shard_map(
        body,
        mesh=mesh,
        in_specs=placed,
        out_specs=(P("seq", "head"), P("seq", "head"), P("seq", "head"), P("seq", "head")),
        check_vma=False,
    )
```

time: 305 us -> 276 us (0.905)
  waiting for transfers between devices: 168 us -> 108 us
  starting transfers between devices: 57.4 us -> 87.1 us
    ppermute x23 -> x32, waiting for transfers between devices: 168 us -> 108 us  [move(): lax.ppermute(value, 'seq', [(a, b) for a, b in pairs if b is not None])]
    ppermute x23 -> x32, starting transfers between devices: 57.3 us -> 87 us  [move(): lax.ppermute(value, 'seq', [(a, b) for a, b in pairs if b is not None])]
    unnamed x47 -> x61, local copies, waits for them, and re-layouts: 8.4 us -> 11 us
  transfers between devices with their start and end apart: 25 -> 34, of which waited for: 12 -> 12; matrix products, arithmetic and copies ran while one was open for 5% -> 6% of each run, Pallas kernels for 12% -> 7%
where the time goes in v2:
time: 276 us; the launch traced here: 274 us
  waiting for transfers between devices  108 us (39%)
  starting transfers between devices  87.1 us (32%)
  Pallas kernels  35.5 us (13%)
  other arithmetic  18.4 us (7%)
  between operations  14.5 us (5%)
  local copies, waits for them, and re-layouts  11.1 us (4%)
    ppermute x32, waiting for transfers between devices, move(): lax.ppermute(value, 'seq', [(a, b) for a, b in pairs if b is not None])  108 us
    ppermute x32, starting transfers between devices, move(): lax.ppermute(value, 'seq', [(a, b) for a, b in pairs if b is not None])  87 us
    unnamed x61, local copies, waits for them, and re-layouts  11 us
    pallas_call x1, Pallas kernels, forward(): pl.pallas_call(forward_kernel, grid_spec=pltpu.PrefetchScalarGridSpec(num...  10.6 us
    pallas_call x1, Pallas kernels, backward(): pl.pallas_call(backward_kernel, grid_spec=pltpu.PrefetchScalarGridSpec(nu...  10.5 us
    pallas_call x1, Pallas kernels, project(): pl.pallas_call(project_kernel, grid=(GROUPS * steps,), in_specs=[pl.Block...  8.61 us
    pallas_call x1, Pallas kernels, project_back(): pl.pallas_call(project_back_kernel, grid=(weight.shape[0] // tile,), in_s...  5.78 us
  transfers between devices with their start and end apart: 34, of which 12 were waited for; matrix products, arithmetic and copies ran while one was open for 6% of the time, Pallas kernels for 7%

profile of v2, /device:TPU:63, one launch (start us, length us, event | category | flops | bytes accessed | tf_op | source)
XLA Modules:
  0.0 274.3 jit_solution(8788495951283589444)
XLA Ops:
  9.1 3.0 %collective-permute-start.9 = (bf16[256,1024]{1,0:T(8,128)(2,1)}, bf16[256,1024]{1,0:T(8,128)(2,1)S(1)}, u32[]{:S(2)}, u32[]{:S(2)}) collective-permute-start(bf16[256,1024]{1,0:T(8,128)(2,1)} %refs_8_.3), channel_id=1, source_target_pairs={{0,64},{4,68},{8,72},{12,76},{16,80},{20,84},{24,88},{28,92},{32,9... | collective-permute-start | bytes 1572872 | tf_op jit(solution)/shard_map/ppermute | solution.py:36
  14.7 10.1 %collective-permute-start.1 = (bf16[256,1024]{1,0:T(8,128)(2,1)}, bf16[256,1024]{1,0:T(8,128)(2,1)S(1)}, u32[]{:S(2)}, u32[]{:S(2)}) collective-permute-start(bf16[256,1024]{1,0:T(8,128)(2,1)} %refs_0_.4), channel_id=1, source_target_pairs={{0,64},{4,68},{8,72},{12,76},{16,80},{20,84},{24,88},{28,92},{32,9... | collective-permute-start | bytes 1572872 | tf_op jit(solution)/shard_map/ppermute | solution.py:36
  28.2 6.3 %collective-permute-done.2.refs_1_ = bf16[256,1024]{1,0:T(8,128)(2,1)S(1)} collective-permute-done((bf16[256,1024]{1,0:T(8,128)(2,1)}, bf16[256,1024]{1,0:T(8,128)(2,1)S(1)}, u32[]{:S(2)}, u32[]{:S(2)}) %collective-permute-start.2) | collective-permute-done | bytes 524320 | tf_op jit(solution)/shard_map/ppermute | solution.py:36
  34.5 12.6 %collective-permute-done.1.refs_0_ = bf16[256,1024]{1,0:T(8,128)(2,1)S(1)} collective-permute-done((bf16[256,1024]{1,0:T(8,128)(2,1)}, bf16[256,1024]{1,0:T(8,128)(2,1)S(1)}, u32[]{:S(2)}, u32[]{:S(2)}) %collective-permute-start.1) | collective-permute-done | bytes 524320 | tf_op jit(solution)/shard_map/ppermute | solution.py:36
  53.5 5.4 %collective-permute-start.5 = (bf16[256,1024]{1,0:T(8,128)(2,1)S(1)}, bf16[256,1024]{1,0:T(8,128)(2,1)S(1)}, u32[]{:S(2)}, u32[]{:S(2)}) collective-permute-start(bf16[256,1024]{1,0:T(8,128)(2,1)S(1)} %copy-done.3), channel_id=1, source_target_pairs={{24,0},{28,4},{56,32},{60,36},{88,64},{92,68},{120,96},{124,100},{... | collective-permute-start | bytes 1572872 | tf_op jit(solution)/shard_map/ppermute | solution.py:36
  61.7 3.0 %collective-permute-done.12 = bf16[256,1024]{1,0:T(8,128)(2,1)} collective-permute-done((bf16[256,1024]{1,0:T(8,128)(2,1)S(1)}, bf16[256,1024]{1,0:T(8,128)(2,1)}, u32[]{:S(2)}, u32[]{:S(2)}) %collective-permute-start.12) | collective-permute-done | bytes 524320 | tf_op jit(solution)/shard_map/ppermute | solution.py:36
  66.6 6.2 %collective-permute-start.13 = (bf16[256,1024]{1,0:T(8,128)(2,1)}, bf16[256,1024]{1,0:T(8,128)(2,1)}, u32[]{:S(2)}, u32[]{:S(2)}) collective-permute-start(bf16[256,1024]{1,0:T(8,128)(2,1)} %broadcast_select_fusion.refs_14_), channel_id=1, source_target_pairs={{24,0},{28,4},{56,32},{60,36},{88,64},{92,68},{120,96},{124,100},{... | collective-permute-start | bytes 1572872 | tf_op jit(solution)/shard_map/ppermute | solution.py:36
  77.2 3.8 %collective-permute-start.14 = (bf16[256,1024]{1,0:T(8,128)(2,1)}, bf16[256,1024]{1,0:T(8,128)(2,1)}, u32[]{:S(2)}, u32[]{:S(2)}) collective-permute-start(bf16[256,1024]{1,0:T(8,128)(2,1)} %broadcast_select_fusion.refs_14_), channel_id=1, source_target_pairs={{16,0},{20,4},{24,8},{28,12},{48,32},{52,36},{56,40},{60,44},{80,6... | collective-permute-start | bytes 1572872 | tf_op jit(solution)/shard_map/ppermute | solution.py:36
  82.3 10.7 %collective-permute-done.13.refs_11_ = bf16[256,1024]{1,0:T(8,128)(2,1)} collective-permute-done((bf16[256,1024]{1,0:T(8,128)(2,1)}, bf16[256,1024]{1,0:T(8,128)(2,1)}, u32[]{:S(2)}, u32[]{:S(2)}) %collective-permute-start.13) | collective-permute-done | bytes 524320 | tf_op jit(solution)/shard_map/ppermute | solution.py:36
  95.2 13.3 %collective-permute-start.15 = (bf16[256,1024]{1,0:T(8,128)(2,1)}, bf16[256,1024]{1,0:T(8,128)(2,1)}, u32[]{:S(2)}, u32[]{:S(2)}) collective-permute-start(bf16[256,1024]{1,0:T(8,128)(2,1)} %after.12), channel_id=1, source_target_pairs={{0,4},{4,0},{8,12},{12,8},{16,20},{20,16},{24,28},{28,24},{32,36},... | collective-permute-start | bytes 1572872 | tf_op jit(solution)/shard_map/ppermute | solution.py:36
  113.5 10.6 %attend.1 = (bf16[8,256,768]{2,1,0:T(8,128)(2,1)}, bf16[256,1024]{1,0:T(8,128)(2,1)S(1)}) custom-call(s32[11]{0:T(128)S(1)} %pad_add_fusion.meta, bf16[256,1024]{1,0:T(8,128)(2,1)S(1)} %copy-done.16, bf16[256,1024]{1,0:T(8,128)(2,1)S(1)} %copy-done.8, bf16[256,1024]{1,0:T(8,128)(2,1)} %collective-permute-done.7.refs_2_.refs_1_, ...), custom_call_target="tpu_custom_call" | custom-call | flops 1000000000 | bytes 9437184 | tf_op jit(solution)/shard_map/attend/pallas_call | solution.py:90
  126.5 5.8 %project_back.1.g = bf16[256,1024]{1,0:T(8,128)(2,1)S(1)} custom-call(bf16[256,4096]{1,0:T(8,128)(2,1)S(1)} %copy-done, bf16[1024,4096]{1,0:T(8,128)(2,1)} %w.3), custom_call_target="tpu_custom_call" | custom-call | flops 2000000000 | bytes 10485760 | tf_op jit(solution)/shard_map/project_back/pallas_call | solution.py:173
  132.4 10.5 %attend_back.1 = (bf16[256,1024]{1,0:T(8,128)(2,1)}, f32[2,256,1024]{2,1,0:T(8,128)}, bf16[2,256,1024]{2,1,0:T(8,128)(2,1)}, bf16[2,256,1024]{2,1,0:T(8,128)(2,1...) custom-call(s32[11]{0:T(128)S(1)} %pad_add_fusion.meta, ...), custom_call_target="tpu_custom_call" | custom-call | flops 2000000000 | bytes 19922944 | tf_op jit(solution)/shard_map/attend_back/pallas_call | solution.py:147
  152.0 4.7 %collective-permute-start.21 = (bf16[256,1024]{1,0:T(8,128)(2,1)}, bf16[256,1024]{1,0:T(8,128)(2,1)S(1)}, u32[]{:S(2)}, u32[]{:S(2)}) collective-permute-start(bf16[256,1024]{1,0:T(8,128)(2,1)} %get-tuple-element.22), channel_id=1, source_target_pairs={{64,0},{68,4},{72,8},{76,12},{80,16},{84,20},{88,24},{92,28},{96,3... | collective-permute-start | bytes 1572872 | tf_op jit(solution)/shard_map/ppermute | solution.py:36
  157.8 8.6 %project.1 = bf16[1024,1024]{1,0:T(8,128)(2,1)} custom-call(bf16[256,1024]{1,0:T(8,128)(2,1)S(1)} %copy-done.6, bf16[1024,4096]{1,0:T(8,128)(2,1)} %w.3), custom_call_target="tpu_custom_call" | custom-call | flops 2000000000 | bytes 11534336 | tf_op jit(solution)/shard_map/project/pallas_call | solution.py:197
  166.4 26.6 %collective-permute-done.20.refs_2_ = bf16[256,1024]{1,0:T(8,128)(2,1)} collective-permute-done((bf16[256,1024]{1,0:T(8,128)(2,1)}, bf16[256,1024]{1,0:T(8,128)(2,1)}, u32[]{:S(2)}, u32[]{:S(2)}) %collective-permute-start.20) | collective-permute-done | bytes 524320 | tf_op jit(solution)/shard_map/ppermute | solution.py:36
  194.3 6.1 %collective-permute-done.25.refs_3_ = bf16[256,1024]{1,0:T(8,128)(2,1)} collective-permute-done((bf16[256,1024]{1,0:T(8,128)(2,1)S(1)}, bf16[256,1024]{1,0:T(8,128)(2,1)}, u32[]{:S(2)}, u32[]{:S(2)}) %collective-permute-start.25) | collective-permute-done | bytes 524320 | tf_op jit(solution)/shard_map/ppermute | solution.py:36
  201.8 7.5 %collective-permute-start.19 = (bf16[2,256,1024]{2,1,0:T(8,128)(2,1)}, bf16[2,256,1024]{2,1,0:T(8,128)(2,1)}, u32[]{:S(2)}, u32[]{:S(2)}) collective-permute-start(bf16[2,256,1024]{2,1,0:T(8,128)(2,1)} %select_add_fusion.refs_1_), channel_id=1, source_target_pairs={{8,0},{12,4},{16,8},{20,12},{24,16},{28,20},{40,32},{44,36},{48,40... | collective-permute-start | bytes 3145736 | tf_op jit(solution)/shard_map/ppermute | solution.py:36
  209.3 3.5 %fusion.10 = (bf16[256,1024]{1,0:T(8,128)(2,1)}, bf16[256,1024]{1,0:T(8,128)(2,1)}) fusion(bf16[256,1024]{1,0:T(8,128)(2,1)} %get-tuple-element.25, bf16[2,256,1024]{2,1,0:T(8,128)(2,1)} %collective-permute-done.23.refs_1_, bf16[2,256,1024]{2,1,0:T(8,128)(2,1)} %after.16, bf16[256,1024]{1,0:T(8,128)(2,1)} %get-tuple-element.23), kind=kLoop, calls=%fused_computation.14 | loop fusion | flops 3145728 | bytes 4194304 | tf_op jit(solution)/shard_map/convert_element_type | solution.py:281
  217.6 6.8 %collective-permute-done.18.refs_1_ = bf16[2,256,1024]{2,1,0:T(8,128)(2,1)S(1)} collective-permute-done((bf16[2,256,1024]{2,1,0:T(8,128)(2,1)}, bf16[2,256,1024]{2,1,0:T(8,128)(2,1)S(1)}, u32[]{:S(2)}, u32[]{:S(2)}) %collective-permute-start.18) | collective-permute-done | bytes 1048608 | tf_op jit(solution)/shard_map/ppermute | solution.py:36
  227.8 19.1 %collective-permute-done.19 = bf16[2,256,1024]{2,1,0:T(8,128)(2,1)} collective-permute-done((bf16[2,256,1024]{2,1,0:T(8,128)(2,1)}, bf16[2,256,1024]{2,1,0:T(8,128)(2,1)}, u32[]{:S(2)}, u32[]{:S(2)}) %collective-permute-start.19) | collective-permute-done | bytes 1048608 | tf_op jit(solution)/shard_map/ppermute | solution.py:36
  246.9 3.0 %convert_add_fusion = f32[2,256,1024]{2,1,0:T(8,128)S(1)} fusion(bf16[2,256,1024]{2,1,0:T(8,128)(2,1)} %collective-permute-done.19, bf16[2,256,1024]{2,1,0:T(8,128)(2,1)} %copy-done.21, f32[2,256,1024]{2,1,0:T(8,128)} %get-tuple-element.20, bf16[2,256,1024]{2,1,0:T(8,128)(2,1)S(1)} %collective-permute-done.17, pred[]{:T(512)S(6)} %eq.14), kind=kLoop, calls=%fused_computation | loop fusion | flops 3670016 | bytes 7340033 | tf_op jit(solution)/shard_map/add | solution.py:287
  250.0 13.8 %collective-permute-done.27 = bf16[256,1024]{1,0:T(8,128)(2,1)} collective-permute-done((bf16[256,1024]{1,0:T(8,128)(2,1)}, bf16[256,1024]{1,0:T(8,128)(2,1)}, u32[]{:S(2)}, u32[]{:S(2)}) %collective-permute-start.27) | collective-permute-done | bytes 524320 | tf_op jit(solution)/shard_map/ppermute | solution.py:36
  263.8 3.7 %fusion.4 = (bf16[256,1024]{1,0:T(8,128)(2,1)}, bf16[256,1024]{1,0:T(8,128)(2,1)}) fusion(f32[2,256,1024]{2,1,0:T(8,128)S(1)} %convert_add_fusion, bf16[256,1024]{1,0:T(8,128)(2,1)S(1)} %collective-permute-done.31, bf16[256,1024]{1,0:T(8,128)(2,1)} %collective-permute-done.29, bf16[256,1024]{1,0:T(8,128)(2,1)S(1)} %copy-done.25, ...), kind=kLoop, calls=%fused_computation.6 | loop fusion | flops 4718592 | bytes 7340032 | tf_op jit(solution)/shard_map/convert_element_type | solution.py:293
  (130 shorter events, 55.1 us)
Async XLA Ops:
  7.2 117.8 %all-gather.2.cloned.1.call-start = ((), (), s32[]{:S(2)}) async-start(), calls=%async_computation.1 | async-start | bytes 2621440 | tf_op jit(solution)/shard_map/all_gather | solution.py:257
  13.4 21.1 %collective-permute-start.2 = (bf16[256,1024]{1,0:T(8,128)(2,1)}, bf16[256,1024]{1,0:T(8,128)(2,1)S(1)}, u32[]{:S(2)}, u32[]{:S(2)}) collective-permute-start(bf16[256,1024]{1,0:T(8,128)(2,1)} %refs_0_.4), channel_id=1, source_target_pairs={{0,32},{4,36},{8,40},{12,44},{16,48},{20,52},{24,56},{28,60},{32,6... | collective-permute-start | bytes 1572872 | tf_op jit(solution)/shard_map/ppermute | solution.py:36
  14.7 32.4 %collective-permute-start.1 = (bf16[256,1024]{1,0:T(8,128)(2,1)}, bf16[256,1024]{1,0:T(8,128)(2,1)S(1)}, u32[]{:S(2)}, u32[]{:S(2)}) collective-permute-start(bf16[256,1024]{1,0:T(8,128)(2,1)} %refs_0_.4), channel_id=1, source_target_pairs={{0,64},{4,68},{8,72},{12,76},{16,80},{20,84},{24,88},{28,92},{32,9... | collective-permute-start | bytes 1572872 | tf_op jit(solution)/shard_map/ppermute | solution.py:36
  24.8 22.2 %collective-permute-start = (bf16[256,1024]{1,0:T(8,128)(2,1)}, bf16[256,1024]{1,0:T(8,128)(2,1)S(1)}, u32[]{:S(2)}, u32[]{:S(2)}) collective-permute-start(bf16[256,1024]{1,0:T(8,128)(2,1)} %refs_0_.4), channel_id=1, source_target_pairs={{0,8},{4,12},{8,16},{12,20},{16,24},{20,28},{32,40},{36,44},{40,48... | collective-permute-start | bytes 1572872 | tf_op jit(solution)/shard_map/ppermute | solution.py:36
  26.2 23.3 %collective-permute-start.10 = (bf16[256,1024]{1,0:T(8,128)(2,1)S(1)}, bf16[256,1024]{1,0:T(8,128)(2,1)}, u32[]{:S(2)}, u32[]{:S(2)}) collective-permute-start(bf16[256,1024]{1,0:T(8,128)(2,1)S(1)} %collective-permute-done.9.refs_15_), channel_id=1, source_target_pairs={{0,128},{4,132},{8,136},{12,140},{16,144},{20,148},{24,152},{28,15... | collective-permute-start | bytes 1572872 | tf_op jit(solution)/shard_map/ppermute | solution.py:36
  50.6 216.9 %reduce-scatter.2.cloned.1.call-start = ((), (), s32[]{:S(2)}) async-start(), calls=%async_computation.2 | async-start | bytes 2621440 | tf_op jit(solution)/shard_map/reduce_scatter | solution.py:274
  53.5 19.2 %collective-permute-start.5 = (bf16[256,1024]{1,0:T(8,128)(2,1)S(1)}, bf16[256,1024]{1,0:T(8,128)(2,1)S(1)}, u32[]{:S(2)}, u32[]{:S(2)}) collective-permute-start(bf16[256,1024]{1,0:T(8,128)(2,1)S(1)} %copy-done.3), channel_id=1, source_target_pairs={{24,0},{28,4},{56,32},{60,36},{88,64},{92,68},{120,96},{124,100},{... | collective-permute-start | bytes 1572872 | tf_op jit(solution)/shard_map/ppermute | solution.py:36
  59.0 23.4 %collective-permute-start.8 = (bf16[256,1024]{1,0:T(8,128)(2,1)S(1)}, bf16[256,1024]{1,0:T(8,128)(2,1)}, u32[]{:S(2)}, u32[]{:S(2)}) collective-permute-start(bf16[256,1024]{1,0:T(8,128)(2,1)S(1)} %copy-done.7), channel_id=1, source_target_pairs={{0,8},{4,12},{8,16},{12,20},{16,24},{20,28},{32,40},{36,44},{40,48... | collective-permute-start | bytes 1572872 | tf_op jit(solution)/shard_map/ppermute | solution.py:36
  66.6 26.4 %collective-permute-start.13 = (bf16[256,1024]{1,0:T(8,128)(2,1)}, bf16[256,1024]{1,0:T(8,128)(2,1)}, u32[]{:S(2)}, u32[]{:S(2)}) collective-permute-start(bf16[256,1024]{1,0:T(8,128)(2,1)} %broadcast_select_fusion.refs_14_), channel_id=1, source_target_pairs={{24,0},{28,4},{56,32},{60,36},{88,64},{92,68},{120,96},{124,100},{... | collective-permute-start | bytes 1572872 | tf_op jit(solution)/shard_map/ppermute | solution.py:36
  74.6 20.6 %collective-permute-start.7 = (bf16[256,1024]{1,0:T(8,128)(2,1)}, bf16[256,1024]{1,0:T(8,128)(2,1)}, u32[]{:S(2)}, u32[]{:S(2)}) collective-permute-start(bf16[256,1024]{1,0:T(8,128)(2,1)} %after.10), channel_id=1, source_target_pairs={{0,4},{4,0},{8,12},{12,8},{16,20},{20,16},{24,28},{28,24},{32,36},... | collective-permute-start | bytes 1572872 | tf_op jit(solution)/shard_map/ppermute | solution.py:36
  77.2 17.9 %collective-permute-start.14 = (bf16[256,1024]{1,0:T(8,128)(2,1)}, bf16[256,1024]{1,0:T(8,128)(2,1)}, u32[]{:S(2)}, u32[]{:S(2)}) collective-permute-start(bf16[256,1024]{1,0:T(8,128)(2,1)} %broadcast_select_fusion.refs_14_), channel_id=1, source_target_pairs={{16,0},{20,4},{24,8},{28,12},{48,32},{52,36},{56,40},{60,44},{80,6... | collective-permute-start | bytes 1572872 | tf_op jit(solution)/shard_map/ppermute | solution.py:36
  81.0 27.6 %collective-permute-start.16 = (bf16[256,1024]{1,0:T(8,128)(2,1)S(1)}, bf16[256,1024]{1,0:T(8,128)(2,1)}, u32[]{:S(2)}, u32[]{:S(2)}) collective-permute-start(bf16[256,1024]{1,0:T(8,128)(2,1)S(1)} %copy-done.7), channel_id=1, source_target_pairs={{0,16},{4,20},{8,24},{12,28},{32,48},{36,52},{40,56},{44,60},{64,8... | collective-permute-start | bytes 1572872 | tf_op jit(solution)/shard_map/ppermute | solution.py:36
  144.0 57.8 %collective-permute-start.23 = (bf16[2,256,1024]{2,1,0:T(8,128)(2,1)}, bf16[2,256,1024]{2,1,0:T(8,128)(2,1)}, u32[]{:S(2)}, u32[]{:S(2)}) collective-permute-start(bf16[2,256,1024]{2,1,0:T(8,128)(2,1)} %get-tuple-element.21), channel_id=1, source_target_pairs={{0,16},{4,20},{8,24},{12,28},{32,48},{36,52},{40,56},{44,60},{64,8... | collective-permute-start | bytes 3145736 | tf_op jit(solution)/shard_map/ppermute | solution.py:36
  148.1 61.2 %collective-permute-start.22 = (bf16[2,256,1024]{2,1,0:T(8,128)(2,1)}, bf16[2,256,1024]{2,1,0:T(8,128)(2,1)}, u32[]{:S(2)}, u32[]{:S(2)}) collective-permute-start(bf16[2,256,1024]{2,1,0:T(8,128)(2,1)} %select_add_fusion.refs_1_), channel_id=1, source_target_pairs={{0,24},{4,28},{32,56},{36,60},{64,88},{68,92},{96,120},{100,124},{... | collective-permute-start | bytes 3145736 | tf_op jit(solution)/shard_map/ppermute | solution.py:36
  149.4 43.6 %collective-permute-start.20 = (bf16[256,1024]{1,0:T(8,128)(2,1)}, bf16[256,1024]{1,0:T(8,128)(2,1)}, u32[]{:S(2)}, u32[]{:S(2)}) collective-permute-start(bf16[256,1024]{1,0:T(8,128)(2,1)} %get-tuple-element.22), channel_id=1, source_target_pairs={{128,64},{132,68},{136,72},{140,76},{144,80},{148,84},{152,88},{15... | collective-permute-start | bytes 1572872 | tf_op jit(solution)/shard_map/ppermute | solution.py:36
  150.7 49.7 %collective-permute-start.25 = (bf16[256,1024]{1,0:T(8,128)(2,1)S(1)}, bf16[256,1024]{1,0:T(8,128)(2,1)}, u32[]{:S(2)}, u32[]{:S(2)}) collective-permute-start(bf16[256,1024]{1,0:T(8,128)(2,1)S(1)} %collective-permute-done.24), channel_id=1, source_target_pairs={{192,64},{196,68},{200,72},{204,76},{208,80},{212,84},{216,88},{22... | collective-permute-start | bytes 1572872 | tf_op jit(solution)/shard_map/ppermute | solution.py:36
  152.0 62.2 %collective-permute-start.21 = (bf16[256,1024]{1,0:T(8,128)(2,1)}, bf16[256,1024]{1,0:T(8,128)(2,1)S(1)}, u32[]{:S(2)}, u32[]{:S(2)}) collective-permute-start(bf16[256,1024]{1,0:T(8,128)(2,1)} %get-tuple-element.22), channel_id=1, source_target_pairs={{64,0},{68,4},{72,8},{76,12},{80,16},{84,20},{88,24},{92,28},{96,3... | collective-permute-start | bytes 1572872 | tf_op jit(solution)/shard_map/ppermute | solution.py:36
  193.0 23.3 %collective-permute-start.28 = (bf16[256,1024]{1,0:T(8,128)(2,1)}, bf16[256,1024]{1,0:T(8,128)(2,1)S(1)}, u32[]{:S(2)}, u32[]{:S(2)}) collective-permute-start(bf16[256,1024]{1,0:T(8,128)(2,1)} %get-tuple-element.24), channel_id=1, source_target_pairs={{64,0},{68,4},{72,8},{76,12},{80,16},{84,20},{88,24},{92,28},{96,3... | collective-permute-start | bytes 1572872 | tf_op jit(solution)/shard_map/ppermute | solution.py:36
  200.4 24.0 %collective-permute-start.18 = (bf16[2,256,1024]{2,1,0:T(8,128)(2,1)}, bf16[2,256,1024]{2,1,0:T(8,128)(2,1)S(1)}, u32[]{:S(2)}, u32[]{:S(2)}) collective-permute-start(bf16[2,256,1024]{2,1,0:T(8,128)(2,1)} %get-tuple-element.21), channel_id=1, source_target_pairs={{16,0},{20,4},{24,8},{28,12},{48,32},{52,36},{56,40},{60,44},{80,6... | collective-permute-start | bytes 3145736 | tf_op jit(solution)/shard_map/ppermute | solution.py:36
  201.8 45.1 %collective-permute-start.19 = (bf16[2,256,1024]{2,1,0:T(8,128)(2,1)}, bf16[2,256,1024]{2,1,0:T(8,128)(2,1)}, u32[]{:S(2)}, u32[]{:S(2)}) collective-permute-start(bf16[2,256,1024]{2,1,0:T(8,128)(2,1)} %select_add_fusion.refs_1_), channel_id=1, source_target_pairs={{8,0},{12,4},{16,8},{20,12},{24,16},{28,20},{40,32},{44,36},{48,40... | collective-permute-start | bytes 3145736 | tf_op jit(solution)/shard_map/ppermute | solution.py:36
  214.3 35.7 %collective-permute-start.29 = (bf16[256,1024]{1,0:T(8,128)(2,1)}, bf16[256,1024]{1,0:T(8,128)(2,1)}, u32[]{:S(2)}, u32[]{:S(2)}) collective-permute-start(bf16[256,1024]{1,0:T(8,128)(2,1)} %get-tuple-element.28), channel_id=1, source_target_pairs={{32,0},{36,4},{40,8},{44,12},{48,16},{52,20},{56,24},{60,28},{64,3... | collective-permute-start | bytes 1572872 | tf_op jit(solution)/shard_map/ppermute | solution.py:36
  216.3 47.4 %collective-permute-start.27 = (bf16[256,1024]{1,0:T(8,128)(2,1)}, bf16[256,1024]{1,0:T(8,128)(2,1)}, u32[]{:S(2)}, u32[]{:S(2)}) collective-permute-start(bf16[256,1024]{1,0:T(8,128)(2,1)} %get-tuple-element.29), channel_id=1, source_target_pairs={{128,96},{132,100},{136,104},{140,108},{144,112},{148,116},{152,12... | collective-permute-start | bytes 1572872 | tf_op jit(solution)/shard_map/ppermute | solution.py:36
  224.4 39.3 %collective-permute-start.26 = (bf16[256,1024]{1,0:T(8,128)(2,1)}, bf16[256,1024]{1,0:T(8,128)(2,1)}, u32[]{:S(2)}, u32[]{:S(2)}) collective-permute-start(bf16[256,1024]{1,0:T(8,128)(2,1)} %get-tuple-element.29), channel_id=1, source_target_pairs={{32,0},{36,4},{40,8},{44,12},{48,16},{52,20},{56,24},{60,28},{64,3... | collective-permute-start | bytes 1572872 | tf_op jit(solution)/shard_map/ppermute | solution.py:36
  226.5 37.2 %collective-permute-start.31 = (bf16[256,1024]{1,0:T(8,128)(2,1)}, bf16[256,1024]{1,0:T(8,128)(2,1)S(1)}, u32[]{:S(2)}, u32[]{:S(2)}) collective-permute-start(bf16[256,1024]{1,0:T(8,128)(2,1)} %after.17), channel_id=1, source_target_pairs={{224,96},{228,100},{232,104},{236,108},{240,112},{244,116},{248,12... | collective-permute-start | bytes 1572872 | tf_op jit(solution)/shard_map/ppermute | solution.py:36
  (40 other events, 421.7 us)
Sparse Core Ops, SparseCore 0:
  50.7 66.1 all-gather.1
  166.6 70.7 reduce-scatter.1

commit v3 on v2

--- a/solution.py
+++ b/solution.py
@@ -257,7 +257,8 @@
     full_grad = lax.all_gather(after(out_grad, v16z, key_set[6]), "head", axis=1, tiled=True)
     value_set = (values,) + wraps(values, *v_roots, v16z, key_set[1]) + (v16a, v16z)
     probs, attended = forward(meta, queries, key_set, value_set)
-    grad_attn = project_back(after(full_grad, attended), out_weight)
+    probs = after(probs, flops=4 * 10**9)
+    grad_attn = project_back(after(full_grad, probs), out_weight)
     dq, own, g1, g2, g4, k8, v8, k16, v16 = backward(
         meta, queries, grad_attn, attended, probs, key_set, value_set
     )

time: 276 us -> 269 us (0.975)
  waiting for transfers between devices: 108 us -> 99.1 us
    ppermute x32, waiting for transfers between devices: 108 us -> 98.2 us  [move(): lax.ppermute(value, 'seq', [(a, b) for a, b in pairs if b is not None])]
  transfers between devices with their start and end apart: 34 -> 34, of which waited for: 12 -> 14; matrix products, arithmetic and copies ran while one was open for 6% -> 7% of each run, Pallas kernels for 7% -> 7%
where the time goes in v3:
time: 269 us; the launch traced here: 268 us
  waiting for transfers between devices  99.1 us (37%)
  starting transfers between devices  89.4 us (33%)
  Pallas kernels  35.5 us (13%)
  other arithmetic  17.5 us (7%)
  between operations  14.5 us (5%)
  local copies, waits for them, and re-layouts  11.7 us (4%)
    ppermute x32, waiting for transfers between devices, move(): lax.ppermute(value, 'seq', [(a, b) for a, b in pairs if b is not None])  98.2 us
    ppermute x32, starting transfers between devices, move(): lax.ppermute(value, 'seq', [(a, b) for a, b in pairs if b is not None])  89.3 us
    unnamed x61, local copies, waits for them, and re-layouts  11.7 us
    pallas_call x1, Pallas kernels, forward(): pl.pallas_call(forward_kernel, grid_spec=pltpu.PrefetchScalarGridSpec(num...  10.6 us
    pallas_call x1, Pallas kernels, backward(): pl.pallas_call(backward_kernel, grid_spec=pltpu.PrefetchScalarGridSpec(nu...  10.5 us
    pallas_call x1, Pallas kernels, project(): pl.pallas_call(project_kernel, grid=(GROUPS * steps,), in_specs=[pl.Block...  8.61 us
    pallas_call x1, Pallas kernels, project_back(): pl.pallas_call(project_back_kernel, grid=(weight.shape[0] // tile,), in_s...  5.79 us
  transfers between devices with their start and end apart: 34, of which 14 were waited for; matrix products, arithmetic and copies ran while one was open for 7% of the time, Pallas kernels for 7%

profile of v3, /device:TPU:63, one launch (start us, length us, event | category | flops | bytes accessed | tf_op | source)
XLA Modules:
  0.0 267.8 jit_solution(10538348530539307858)
XLA Ops:
  14.7 10.1 %collective-permute-start.1 = (bf16[256,1024]{1,0:T(8,128)(2,1)}, bf16[256,1024]{1,0:T(8,128)(2,1)S(1)}, u32[]{:S(2)}, u32[]{:S(2)}) collective-permute-start(bf16[256,1024]{1,0:T(8,128)(2,1)} %refs_0_.4), channel_id=1, source_target_pairs={{0,64},{4,68},{8,72},{12,76},{16,80},{20,84},{24,88},{28,92},{32,9... | collective-permute-start | bytes 1572872 | tf_op jit(solution)/shard_map/ppermute | solution.py:36
  29.5 5.0 %collective-permute-done.2.refs_1_ = bf16[256,1024]{1,0:T(8,128)(2,1)S(1)} collective-permute-done((bf16[256,1024]{1,0:T(8,128)(2,1)}, bf16[256,1024]{1,0:T(8,128)(2,1)S(1)}, u32[]{:S(2)}, u32[]{:S(2)}) %collective-permute-start.2) | collective-permute-done | bytes 524320 | tf_op jit(solution)/shard_map/ppermute | solution.py:36
  34.5 12.6 %collective-permute-done.1.refs_0_ = bf16[256,1024]{1,0:T(8,128)(2,1)S(1)} collective-permute-done((bf16[256,1024]{1,0:T(8,128)(2,1)}, bf16[256,1024]{1,0:T(8,128)(2,1)S(1)}, u32[]{:S(2)}, u32[]{:S(2)}) %collective-permute-start.1) | collective-permute-done | bytes 524320 | tf_op jit(solution)/shard_map/ppermute | solution.py:36
  52.0 5.6 %collective-permute-start.5 = (bf16[256,1024]{1,0:T(8,128)(2,1)S(1)}, bf16[256,1024]{1,0:T(8,128)(2,1)S(1)}, u32[]{:S(2)}, u32[]{:S(2)}) collective-permute-start(bf16[256,1024]{1,0:T(8,128)(2,1)S(1)} %broadcast_select_fusion.1.refs_6_.refs_2_), channel_id=1, source_target_pairs={{24,0},{28,4},{56,32},{60,36},{88,64},{92,68},{120,96},{124,100},{... | collective-permute-start | bytes 1572872 | tf_op jit(solution)/shard_map/ppermute | solution.py:36
  62.4 3.1 %collective-permute-start.13 = (bf16[256,1024]{1,0:T(8,128)(2,1)}, bf16[256,1024]{1,0:T(8,128)(2,1)}, u32[]{:S(2)}, u32[]{:S(2)}) collective-permute-start(bf16[256,1024]{1,0:T(8,128)(2,1)} %broadcast_select_fusion.refs_14_), channel_id=1, source_target_pairs={{24,0},{28,4},{56,32},{60,36},{88,64},{92,68},{120,96},{124,100},{... | collective-permute-start | bytes 1572872 | tf_op jit(solution)/shard_map/ppermute | solution.py:36
  73.8 6.1 %collective-permute-start.14 = (bf16[256,1024]{1,0:T(8,128)(2,1)}, bf16[256,1024]{1,0:T(8,128)(2,1)}, u32[]{:S(2)}, u32[]{:S(2)}) collective-permute-start(bf16[256,1024]{1,0:T(8,128)(2,1)} %broadcast_select_fusion.refs_14_), channel_id=1, source_target_pairs={{16,0},{20,4},{24,8},{28,12},{48,32},{52,36},{56,40},{60,44},{80,6... | collective-permute-start | bytes 1572872 | tf_op jit(solution)/shard_map/ppermute | solution.py:36
  81.2 8.6 %collective-permute-done.13.refs_11_ = bf16[256,1024]{1,0:T(8,128)(2,1)} collective-permute-done((bf16[256,1024]{1,0:T(8,128)(2,1)}, bf16[256,1024]{1,0:T(8,128)(2,1)}, u32[]{:S(2)}, u32[]{:S(2)}) %collective-permute-start.13) | collective-permute-done | bytes 524320 | tf_op jit(solution)/shard_map/ppermute | solution.py:36
  91.9 13.7 %collective-permute-start.15 = (bf16[256,1024]{1,0:T(8,128)(2,1)}, bf16[256,1024]{1,0:T(8,128)(2,1)}, u32[]{:S(2)}, u32[]{:S(2)}) collective-permute-start(bf16[256,1024]{1,0:T(8,128)(2,1)} %after.13), channel_id=1, source_target_pairs={{0,4},{4,0},{8,12},{12,8},{16,20},{20,16},{24,28},{28,24},{32,36},... | collective-permute-start | bytes 1572872 | tf_op jit(solution)/shard_map/ppermute | solution.py:36
  110.7 10.6 %attend.1 = (bf16[8,256,768]{2,1,0:T(8,128)(2,1)}, bf16[256,1024]{1,0:T(8,128)(2,1)S(1)}) custom-call(s32[11]{0:T(128)S(1)} %pad_add_fusion.meta, bf16[256,1024]{1,0:T(8,128)(2,1)S(1)} %copy-done.15, bf16[256,1024]{1,0:T(8,128)(2,1)S(1)} %copy-done.6, bf16[256,1024]{1,0:T(8,128)(2,1)} %collective-permute-done.7.refs_2_.refs_1_, ...), custom_call_target="tpu_custom_call" | custom-call | flops 1000000000 | bytes 9437184 | tf_op jit(solution)/shard_map/attend/pallas_call | solution.py:90
  124.5 5.8 %project_back.1.g = bf16[256,1024]{1,0:T(8,128)(2,1)S(1)} custom-call(bf16[256,4096]{1,0:T(8,128)(2,1)S(1)} %copy-done, bf16[1024,4096]{1,0:T(8,128)(2,1)} %w.3), custom_call_target="tpu_custom_call" | custom-call | flops 2000000000 | bytes 10485760 | tf_op jit(solution)/shard_map/project_back/pallas_call | solution.py:173
  130.3 10.5 %attend_back.1 = (bf16[256,1024]{1,0:T(8,128)(2,1)}, f32[2,256,1024]{2,1,0:T(8,128)}, bf16[2,256,1024]{2,1,0:T(8,128)(2,1)}, bf16[2,256,1024]{2,1,0:T(8,128)(2,1...) custom-call(s32[11]{0:T(128)S(1)} %pad_add_fusion.meta, ...), custom_call_target="tpu_custom_call" | custom-call | flops 2000000000 | bytes 19922944 | tf_op jit(solution)/shard_map/attend_back/pallas_call | solution.py:147
  151.5 3.4 %collective-permute-start.21 = (bf16[256,1024]{1,0:T(8,128)(2,1)}, bf16[256,1024]{1,0:T(8,128)(2,1)S(1)}, u32[]{:S(2)}, u32[]{:S(2)}) collective-permute-start(bf16[256,1024]{1,0:T(8,128)(2,1)} %get-tuple-element.22), channel_id=1, source_target_pairs={{64,0},{68,4},{72,8},{76,12},{80,16},{84,20},{88,24},{92,28},{96,3... | collective-permute-start | bytes 1572872 | tf_op jit(solution)/shard_map/ppermute | solution.py:36
  156.0 8.6 %project.1 = bf16[1024,1024]{1,0:T(8,128)(2,1)} custom-call(bf16[256,1024]{1,0:T(8,128)(2,1)S(1)} %copy-done.14, bf16[1024,4096]{1,0:T(8,128)(2,1)} %w.3), custom_call_target="tpu_custom_call" | custom-call | flops 2000000000 | bytes 11534336 | tf_op jit(solution)/shard_map/project/pallas_call | solution.py:197
  164.6 19.3 %collective-permute-done.20.refs_2_ = bf16[256,1024]{1,0:T(8,128)(2,1)} collective-permute-done((bf16[256,1024]{1,0:T(8,128)(2,1)}, bf16[256,1024]{1,0:T(8,128)(2,1)}, u32[]{:S(2)}, u32[]{:S(2)}) %collective-permute-start.20) | collective-permute-done | bytes 524320 | tf_op jit(solution)/shard_map/ppermute | solution.py:36
  185.2 6.1 %collective-permute-done.25.refs_3_ = bf16[256,1024]{1,0:T(8,128)(2,1)} collective-permute-done((bf16[256,1024]{1,0:T(8,128)(2,1)S(1)}, bf16[256,1024]{1,0:T(8,128)(2,1)}, u32[]{:S(2)}, u32[]{:S(2)}) %collective-permute-start.25) | collective-permute-done | bytes 524320 | tf_op jit(solution)/shard_map/ppermute | solution.py:36
  192.7 7.3 %collective-permute-start.19 = (bf16[2,256,1024]{2,1,0:T(8,128)(2,1)}, bf16[2,256,1024]{2,1,0:T(8,128)(2,1)}, u32[]{:S(2)}, u32[]{:S(2)}) collective-permute-start(bf16[2,256,1024]{2,1,0:T(8,128)(2,1)} %select_add_fusion.refs_1_), channel_id=1, source_target_pairs={{8,0},{12,4},{16,8},{20,12},{24,16},{28,20},{40,32},{44,36},{48,40... | collective-permute-start | bytes 3145736 | tf_op jit(solution)/shard_map/ppermute | solution.py:36
  200.0 3.5 %fusion.10 = (bf16[256,1024]{1,0:T(8,128)(2,1)}, bf16[256,1024]{1,0:T(8,128)(2,1)}) fusion(bf16[256,1024]{1,0:T(8,128)(2,1)} %get-tuple-element.25, bf16[2,256,1024]{2,1,0:T(8,128)(2,1)} %collective-permute-done.23.refs_1_, bf16[2,256,1024]{2,1,0:T(8,128)(2,1)} %after.18, bf16[256,1024]{1,0:T(8,128)(2,1)} %get-tuple-element.23), kind=kLoop, calls=%fused_computation.14 | loop fusion | flops 3145728 | bytes 4194304 | tf_op jit(solution)/shard_map/convert_element_type | solution.py:282
  204.9 4.2 %collective-permute-start.29 = (bf16[256,1024]{1,0:T(8,128)(2,1)}, bf16[256,1024]{1,0:T(8,128)(2,1)}, u32[]{:S(2)}, u32[]{:S(2)}) collective-permute-start(bf16[256,1024]{1,0:T(8,128)(2,1)} %get-tuple-element.28), channel_id=1, source_target_pairs={{32,0},{36,4},{40,8},{44,12},{48,16},{52,20},{56,24},{60,28},{64,3... | collective-permute-start | bytes 1572872 | tf_op jit(solution)/shard_map/ppermute | solution.py:36
  210.4 4.9 %collective-permute-done.18.refs_1_ = bf16[2,256,1024]{2,1,0:T(8,128)(2,1)S(1)} collective-permute-done((bf16[2,256,1024]{2,1,0:T(8,128)(2,1)}, bf16[2,256,1024]{2,1,0:T(8,128)(2,1)S(1)}, u32[]{:S(2)}, u32[]{:S(2)}) %collective-permute-start.18) | collective-permute-done | bytes 1048608 | tf_op jit(solution)/shard_map/ppermute | solution.py:36
  215.3 3.4 %collective-permute-start.26 = (bf16[256,1024]{1,0:T(8,128)(2,1)}, bf16[256,1024]{1,0:T(8,128)(2,1)}, u32[]{:S(2)}, u32[]{:S(2)}) collective-permute-start(bf16[256,1024]{1,0:T(8,128)(2,1)} %get-tuple-element.29), channel_id=1, source_target_pairs={{32,0},{36,4},{40,8},{44,12},{48,16},{52,20},{56,24},{60,28},{64,3... | collective-permute-start | bytes 1572872 | tf_op jit(solution)/shard_map/ppermute | solution.py:36
  220.1 17.7 %collective-permute-done.19 = bf16[2,256,1024]{2,1,0:T(8,128)(2,1)} collective-permute-done((bf16[2,256,1024]{2,1,0:T(8,128)(2,1)}, bf16[2,256,1024]{2,1,0:T(8,128)(2,1)}, u32[]{:S(2)}, u32[]{:S(2)}) %collective-permute-start.19) | collective-permute-done | bytes 1048608 | tf_op jit(solution)/shard_map/ppermute | solution.py:36
  237.8 3.0 %convert_add_fusion = f32[2,256,1024]{2,1,0:T(8,128)S(1)} fusion(bf16[2,256,1024]{2,1,0:T(8,128)(2,1)} %collective-permute-done.19, bf16[2,256,1024]{2,1,0:T(8,128)(2,1)} %copy-done.21, f32[2,256,1024]{2,1,0:T(8,128)} %get-tuple-element.20, bf16[2,256,1024]{2,1,0:T(8,128)(2,1)S(1)} %collective-permute-done.17, pred[]{:T(512)S(6)} %eq.14), kind=kLoop, calls=%fused_computation | loop fusion | flops 3670016 | bytes 7340033 | tf_op jit(solution)/shard_map/add | solution.py:288
  240.9 16.3 %collective-permute-done.27 = bf16[256,1024]{1,0:T(8,128)(2,1)} collective-permute-done((bf16[256,1024]{1,0:T(8,128)(2,1)}, bf16[256,1024]{1,0:T(8,128)(2,1)}, u32[]{:S(2)}, u32[]{:S(2)}) %collective-permute-start.27) | collective-permute-done | bytes 524320 | tf_op jit(solution)/shard_map/ppermute | solution.py:36
  257.2 3.7 %fusion.4 = (bf16[256,1024]{1,0:T(8,128)(2,1)}, bf16[256,1024]{1,0:T(8,128)(2,1)}) fusion(f32[2,256,1024]{2,1,0:T(8,128)S(1)} %convert_add_fusion, bf16[256,1024]{1,0:T(8,128)(2,1)S(1)} %collective-permute-done.31, bf16[256,1024]{1,0:T(8,128)(2,1)} %collective-permute-done.29, bf16[256,1024]{1,0:T(8,128)(2,1)S(1)} %copy-done.25, ...), kind=kLoop, calls=%fused_computation.6 | loop fusion | flops 4718592 | bytes 7340032 | tf_op jit(solution)/shard_map/convert_element_type | solution.py:294
  (131 shorter events, 60.1 us)
Async XLA Ops:
  7.2 115.7 %all-gather.2.cloned.1.call-start = ((), (), s32[]{:S(2)}) async-start(), calls=%async_computation.1 | async-start | bytes 2621440 | tf_op jit(solution)/shard_map/all_gather | solution.py:257
  13.4 21.1 %collective-permute-start.2 = (bf16[256,1024]{1,0:T(8,128)(2,1)}, bf16[256,1024]{1,0:T(8,128)(2,1)S(1)}, u32[]{:S(2)}, u32[]{:S(2)}) collective-permute-start(bf16[256,1024]{1,0:T(8,128)(2,1)} %refs_0_.4), channel_id=1, source_target_pairs={{0,32},{4,36},{8,40},{12,44},{16,48},{20,52},{24,56},{28,60},{32,6... | collective-permute-start | bytes 1572872 | tf_op jit(solution)/shard_map/ppermute | solution.py:36
  14.7 32.4 %collective-permute-start.1 = (bf16[256,1024]{1,0:T(8,128)(2,1)}, bf16[256,1024]{1,0:T(8,128)(2,1)S(1)}, u32[]{:S(2)}, u32[]{:S(2)}) collective-permute-start(bf16[256,1024]{1,0:T(8,128)(2,1)} %refs_0_.4), channel_id=1, source_target_pairs={{0,64},{4,68},{8,72},{12,76},{16,80},{20,84},{24,88},{28,92},{32,9... | collective-permute-start | bytes 1572872 | tf_op jit(solution)/shard_map/ppermute | solution.py:36
  24.8 22.2 %collective-permute-start = (bf16[256,1024]{1,0:T(8,128)(2,1)}, bf16[256,1024]{1,0:T(8,128)(2,1)S(1)}, u32[]{:S(2)}, u32[]{:S(2)}) collective-permute-start(bf16[256,1024]{1,0:T(8,128)(2,1)} %refs_0_.4), channel_id=1, source_target_pairs={{0,8},{4,12},{8,16},{12,20},{16,24},{20,28},{32,40},{36,44},{40,48... | collective-permute-start | bytes 1572872 | tf_op jit(solution)/shard_map/ppermute | solution.py:36
  26.2 23.3 %collective-permute-start.10 = (bf16[256,1024]{1,0:T(8,128)(2,1)S(1)}, bf16[256,1024]{1,0:T(8,128)(2,1)S(1)}, u32[]{:S(2)}, u32[]{:S(2)}) collective-permute-start(bf16[256,1024]{1,0:T(8,128)(2,1)S(1)} %collective-permute-done.9.refs_15_), channel_id=1, source_target_pairs={{0,128},{4,132},{8,136},{12,140},{16,144},{20,148},{24,152},{28,15... | collective-permute-start | bytes 1572872 | tf_op jit(solution)/shard_map/ppermute | solution.py:36
  28.2 32.2 %collective-permute-start.12 = (bf16[256,1024]{1,0:T(8,128)(2,1)}, bf16[256,1024]{1,0:T(8,128)(2,1)}, u32[]{:S(2)}, u32[]{:S(2)}) collective-permute-start(bf16[256,1024]{1,0:T(8,128)(2,1)} %refs_8_.3), channel_id=1, source_target_pairs={{0,32},{4,36},{8,40},{12,44},{16,48},{20,52},{24,56},{28,60},{32,6... | collective-permute-start | bytes 1572872 | tf_op jit(solution)/shard_map/ppermute | solution.py:36
  57.6 203.3 %reduce-scatter.2.cloned.1.call-start = ((), (), s32[]{:S(2)}) async-start(), calls=%async_computation.2 | async-start | bytes 2621440 | tf_op jit(solution)/shard_map/reduce_scatter | solution.py:275
  57.7 23.6 %collective-permute-start.8 = (bf16[256,1024]{1,0:T(8,128)(2,1)S(1)}, bf16[256,1024]{1,0:T(8,128)(2,1)}, u32[]{:S(2)}, u32[]{:S(2)}) collective-permute-start(bf16[256,1024]{1,0:T(8,128)(2,1)S(1)} %copy-done.5), channel_id=1, source_target_pairs={{0,8},{4,12},{8,16},{12,20},{16,24},{20,28},{32,40},{36,44},{40,48... | collective-permute-start | bytes 1572872 | tf_op jit(solution)/shard_map/ppermute | solution.py:36
  62.4 27.5 %collective-permute-start.13 = (bf16[256,1024]{1,0:T(8,128)(2,1)}, bf16[256,1024]{1,0:T(8,128)(2,1)}, u32[]{:S(2)}, u32[]{:S(2)}) collective-permute-start(bf16[256,1024]{1,0:T(8,128)(2,1)} %broadcast_select_fusion.refs_14_), channel_id=1, source_target_pairs={{24,0},{28,4},{56,32},{60,36},{88,64},{92,68},{120,96},{124,100},{... | collective-permute-start | bytes 1572872 | tf_op jit(solution)/shard_map/ppermute | solution.py:36
  71.2 20.7 %collective-permute-start.7 = (bf16[256,1024]{1,0:T(8,128)(2,1)}, bf16[256,1024]{1,0:T(8,128)(2,1)}, u32[]{:S(2)}, u32[]{:S(2)}) collective-permute-start(bf16[256,1024]{1,0:T(8,128)(2,1)} %after.11), channel_id=1, source_target_pairs={{0,4},{4,0},{8,12},{12,8},{16,20},{20,16},{24,28},{28,24},{32,36},... | collective-permute-start | bytes 1572872 | tf_op jit(solution)/shard_map/ppermute | solution.py:36
  73.8 18.1 %collective-permute-start.14 = (bf16[256,1024]{1,0:T(8,128)(2,1)}, bf16[256,1024]{1,0:T(8,128)(2,1)}, u32[]{:S(2)}, u32[]{:S(2)}) collective-permute-start(bf16[256,1024]{1,0:T(8,128)(2,1)} %broadcast_select_fusion.refs_14_), channel_id=1, source_target_pairs={{16,0},{20,4},{24,8},{28,12},{48,32},{52,36},{56,40},{60,44},{80,6... | collective-permute-start | bytes 1572872 | tf_op jit(solution)/shard_map/ppermute | solution.py:36
  79.9 25.9 %collective-permute-start.16 = (bf16[256,1024]{1,0:T(8,128)(2,1)S(1)}, bf16[256,1024]{1,0:T(8,128)(2,1)}, u32[]{:S(2)}, u32[]{:S(2)}) collective-permute-start(bf16[256,1024]{1,0:T(8,128)(2,1)S(1)} %copy-done.5), channel_id=1, source_target_pairs={{0,16},{4,20},{8,24},{12,28},{32,48},{36,52},{40,56},{44,60},{64,8... | collective-permute-start | bytes 1572872 | tf_op jit(solution)/shard_map/ppermute | solution.py:36
  143.5 49.2 %collective-permute-start.23 = (bf16[2,256,1024]{2,1,0:T(8,128)(2,1)}, bf16[2,256,1024]{2,1,0:T(8,128)(2,1)}, u32[]{:S(2)}, u32[]{:S(2)}) collective-permute-start(bf16[2,256,1024]{2,1,0:T(8,128)(2,1)} %get-tuple-element.21), channel_id=1, source_target_pairs={{0,16},{4,20},{8,24},{12,28},{32,48},{36,52},{40,56},{44,60},{64,8... | collective-permute-start | bytes 3145736 | tf_op jit(solution)/shard_map/ppermute | solution.py:36
  147.6 52.3 %collective-permute-start.22 = (bf16[2,256,1024]{2,1,0:T(8,128)(2,1)}, bf16[2,256,1024]{2,1,0:T(8,128)(2,1)}, u32[]{:S(2)}, u32[]{:S(2)}) collective-permute-start(bf16[2,256,1024]{2,1,0:T(8,128)(2,1)} %select_add_fusion.refs_1_), channel_id=1, source_target_pairs={{0,24},{4,28},{32,56},{36,60},{64,88},{68,92},{96,120},{100,124},{... | collective-permute-start | bytes 3145736 | tf_op jit(solution)/shard_map/ppermute | solution.py:36
  148.9 35.0 %collective-permute-start.20 = (bf16[256,1024]{1,0:T(8,128)(2,1)}, bf16[256,1024]{1,0:T(8,128)(2,1)}, u32[]{:S(2)}, u32[]{:S(2)}) collective-permute-start(bf16[256,1024]{1,0:T(8,128)(2,1)} %get-tuple-element.22), channel_id=1, source_target_pairs={{128,64},{132,68},{136,72},{140,76},{144,80},{148,84},{152,88},{15... | collective-permute-start | bytes 1572872 | tf_op jit(solution)/shard_map/ppermute | solution.py:36
  150.2 41.1 %collective-permute-start.25 = (bf16[256,1024]{1,0:T(8,128)(2,1)S(1)}, bf16[256,1024]{1,0:T(8,128)(2,1)}, u32[]{:S(2)}, u32[]{:S(2)}) collective-permute-start(bf16[256,1024]{1,0:T(8,128)(2,1)S(1)} %collective-permute-done.24), channel_id=1, source_target_pairs={{192,64},{196,68},{200,72},{204,76},{208,80},{212,84},{216,88},{22... | collective-permute-start | bytes 1572872 | tf_op jit(solution)/shard_map/ppermute | solution.py:36
  151.5 53.4 %collective-permute-start.21 = (bf16[256,1024]{1,0:T(8,128)(2,1)}, bf16[256,1024]{1,0:T(8,128)(2,1)S(1)}, u32[]{:S(2)}, u32[]{:S(2)}) collective-permute-start(bf16[256,1024]{1,0:T(8,128)(2,1)} %get-tuple-element.22), channel_id=1, source_target_pairs={{64,0},{68,4},{72,8},{76,12},{80,16},{84,20},{88,24},{92,28},{96,3... | collective-permute-start | bytes 1572872 | tf_op jit(solution)/shard_map/ppermute | solution.py:36
  183.9 25.2 %collective-permute-start.28 = (bf16[256,1024]{1,0:T(8,128)(2,1)}, bf16[256,1024]{1,0:T(8,128)(2,1)S(1)}, u32[]{:S(2)}, u32[]{:S(2)}) collective-permute-start(bf16[256,1024]{1,0:T(8,128)(2,1)} %get-tuple-element.24), channel_id=1, source_target_pairs={{64,0},{68,4},{72,8},{76,12},{80,16},{84,20},{88,24},{92,28},{96,3... | collective-permute-start | bytes 1572872 | tf_op jit(solution)/shard_map/ppermute | solution.py:36
  191.3 24.0 %collective-permute-start.18 = (bf16[2,256,1024]{2,1,0:T(8,128)(2,1)}, bf16[2,256,1024]{2,1,0:T(8,128)(2,1)S(1)}, u32[]{:S(2)}, u32[]{:S(2)}) collective-permute-start(bf16[2,256,1024]{2,1,0:T(8,128)(2,1)} %get-tuple-element.21), channel_id=1, source_target_pairs={{16,0},{20,4},{24,8},{28,12},{48,32},{52,36},{56,40},{60,44},{80,6... | collective-permute-start | bytes 3145736 | tf_op jit(solution)/shard_map/ppermute | solution.py:36
  192.7 45.1 %collective-permute-start.19 = (bf16[2,256,1024]{2,1,0:T(8,128)(2,1)}, bf16[2,256,1024]{2,1,0:T(8,128)(2,1)}, u32[]{:S(2)}, u32[]{:S(2)}) collective-permute-start(bf16[2,256,1024]{2,1,0:T(8,128)(2,1)} %select_add_fusion.refs_1_), channel_id=1, source_target_pairs={{8,0},{12,4},{16,8},{20,12},{24,16},{28,20},{40,32},{44,36},{48,40... | collective-permute-start | bytes 3145736 | tf_op jit(solution)/shard_map/ppermute | solution.py:36
  204.9 36.0 %collective-permute-start.29 = (bf16[256,1024]{1,0:T(8,128)(2,1)}, bf16[256,1024]{1,0:T(8,128)(2,1)}, u32[]{:S(2)}, u32[]{:S(2)}) collective-permute-start(bf16[256,1024]{1,0:T(8,128)(2,1)} %get-tuple-element.28), channel_id=1, source_target_pairs={{32,0},{36,4},{40,8},{44,12},{48,16},{52,20},{56,24},{60,28},{64,3... | collective-permute-start | bytes 1572872 | tf_op jit(solution)/shard_map/ppermute | solution.py:36
  209.1 48.1 %collective-permute-start.27 = (bf16[256,1024]{1,0:T(8,128)(2,1)}, bf16[256,1024]{1,0:T(8,128)(2,1)}, u32[]{:S(2)}, u32[]{:S(2)}) collective-permute-start(bf16[256,1024]{1,0:T(8,128)(2,1)} %get-tuple-element.29), channel_id=1, source_target_pairs={{128,96},{132,100},{136,104},{140,108},{144,112},{148,116},{152,12... | collective-permute-start | bytes 1572872 | tf_op jit(solution)/shard_map/ppermute | solution.py:36
  215.3 41.8 %collective-permute-start.26 = (bf16[256,1024]{1,0:T(8,128)(2,1)}, bf16[256,1024]{1,0:T(8,128)(2,1)}, u32[]{:S(2)}, u32[]{:S(2)}) collective-permute-start(bf16[256,1024]{1,0:T(8,128)(2,1)} %get-tuple-element.29), channel_id=1, source_target_pairs={{32,0},{36,4},{40,8},{44,12},{48,16},{52,20},{56,24},{60,28},{64,3... | collective-permute-start | bytes 1572872 | tf_op jit(solution)/shard_map/ppermute | solution.py:36
  218.8 38.4 %collective-permute-start.31 = (bf16[256,1024]{1,0:T(8,128)(2,1)}, bf16[256,1024]{1,0:T(8,128)(2,1)S(1)}, u32[]{:S(2)}, u32[]{:S(2)}) collective-permute-start(bf16[256,1024]{1,0:T(8,128)(2,1)} %after.19), channel_id=1, source_target_pairs={{224,96},{228,100},{232,104},{236,108},{240,112},{244,116},{248,12... | collective-permute-start | bytes 1572872 | tf_op jit(solution)/shard_map/ppermute | solution.py:36
  (40 other events, 424.4 us)
Sparse Core Ops, SparseCore 0:
  57.7 65.1 all-gather.1
  164.8 66.0 reduce-scatter.1
